TPU v7x, 512 devices: a whole 4x8x8 slice. The times are simulated.
512 devices in a mesh: seq: 128 (over x, y_lo, z, core), tp: 4 (over y_hi).
Axes of the slice: x: 4, y: 8 (y_hi: 4, y_lo: 2; y = y_hi * 2 + y_lo), z: 8, core: 2. Of those that a mesh axis runs over, the one named last changes fastest.
Arguments:
- queries: bfloat16 [16384, 5120], P('seq', 'tp'), may hold values from -72 to 72
- keys: bfloat16 [16384, 5120], P('seq', 'tp'), may hold values from -72 to 72
- values: bfloat16 [16384, 5120], P('seq', 'tp'), may hold values from -6 to 6
- query_gain: float32 [5120], P('tp'), may hold values from 0.1 to 1.9
- key_gain: float32 [5120], P('tp'), may hold values from 0.1 to 1.9
Outputs:
- mixed: bfloat16 [16384, 5120], P('seq', 'tp')
All inputs are finite; a program needn't handle non-finite values.
Results may differ from a plain program's by a relative error of at most 0.0077.
Values may be sent and summed in bfloat16 or wider, within the bound.
No kernel may reach another device: no remote copies, remote signals or barrier semaphores. Data moves between devices by JAX's collectives and lax.ppermute only.
A program may use at most 64 MiB of HBM per device.

v0:
```python
import math

import jax
import jax.numpy as jnp
from jax import lax
from jax.sharding import PartitionSpec as P

D = 5120
HEAD_DIM = 128


def swapped(value, axis, bit):
    mask = 2**bit
    pairs = [(source, source ^ mask) for source in range(lax.axis_size(axis))]
    return lax.ppermute(value, axis, pairs)


def normalize(block_in, sum_sq, gain_vec):
    scale = lax.rsqrt(sum_sq / D + 1e-06)
    return (block_in.astype(jnp.float32) * scale[:, None] * gain_vec[None, :]).astype(jnp.bfloat16)


def one_head(triple):
    q_head, k_head, v_head = triple
    scores = jnp.dot(q_head, k_head.T, preferred_element_type=jnp.float32) / math.sqrt(
        q_head.shape[-1]
    )
    top_score = jnp.max(scores, axis=-1, keepdims=True)
    raised = jnp.exp(scores - top_score)
    weights = (raised / jnp.sum(raised, axis=-1, keepdims=True)).astype(jnp.bfloat16)
    return jnp.dot(weights, v_head, preferred_element_type=jnp.float32)


def temporal_mix(pieces, group):
    q_in, k_in, v_in = pieces
    senders, per_dev, heads_in, head_dim = q_in.shape

    def regroup(array_in):
        return array_in.reshape(senders // group, group * per_dev, heads_in, head_dim)

    scores = jnp.einsum(
        "fahe,gahe->ahfg", regroup(q_in), regroup(k_in), preferred_element_type=jnp.float32
    ) / math.sqrt(head_dim)
    top_score = jnp.max(scores, axis=-1, keepdims=True)
    raised = jnp.exp(scores - top_score)
    weights = (raised / jnp.sum(raised, axis=-1, keepdims=True)).astype(jnp.bfloat16)
    result = jnp.einsum(
        "ahfg,gahe->fahe", weights, regroup(v_in), preferred_element_type=jnp.float32
    )
    return result.astype(jnp.bfloat16).reshape(senders, per_dev, heads_in, head_dim)


def per_device(queries, keys, values, query_gain, key_gain):
    tok_rows, col_width = queries.shape
    head_count = col_width // HEAD_DIM
    group = min(8, lax.axis_size("seq") // 2)
    part_q = jnp.sum(jnp.square(queries.astype(jnp.float32)), axis=1)
    part_k = jnp.sum(jnp.square(keys.astype(jnp.float32)), axis=1)
    sum_q, sum_k = lax.psum((part_q, part_k), "tp")
    q_norm = normalize(queries, sum_q, query_gain)
    k_norm = normalize(keys, sum_k, key_gain)
    my_index = lax.axis_index("seq")
    frame_k, frame_v = (k_norm, values)
    for bit in range(group.bit_length() - 1):
        other_k, other_v = swapped((frame_k, frame_v), "seq", bit)
        is_lower = my_index >> bit & 1 == 0
        frame_k = jnp.where(
            is_lower,
            jnp.concatenate([frame_k, other_k], axis=0),
            jnp.concatenate([other_k, frame_k], axis=0),
        )
        frame_v = jnp.where(
            is_lower,
            jnp.concatenate([frame_v, other_v], axis=0),
            jnp.concatenate([other_v, frame_v], axis=0),
        )
    frame_len = frame_k.shape[0]
    q_heads = q_norm.reshape(tok_rows, head_count, HEAD_DIM).transpose(1, 0, 2)
    k_heads = frame_k.reshape(frame_len, head_count, HEAD_DIM).transpose(1, 0, 2)
    v_heads = frame_v.reshape(frame_len, head_count, HEAD_DIM).transpose(1, 0, 2)
    spatial = lax.map(one_head, (q_heads, k_heads, v_heads)).transpose(1, 0, 2)
    q_four = q_norm.reshape(1, tok_rows, head_count, HEAD_DIM)
    k_four = k_norm.reshape(1, tok_rows, head_count, HEAD_DIM)
    v_four = values.reshape(1, tok_rows, head_count, HEAD_DIM)
    switched = (
        lax.all_to_all(q_four, "seq", split_axis=1, concat_axis=0, tiled=True),
        lax.all_to_all(k_four, "seq", split_axis=1, concat_axis=0, tiled=True),
        lax.all_to_all(v_four, "seq", split_axis=1, concat_axis=0, tiled=True),
    )
    returned = lax.all_to_all(
        temporal_mix(switched, group), "seq", split_axis=0, concat_axis=1, tiled=True
    )
    summed = spatial + returned[0].astype(jnp.float32)
    return summed.reshape(tok_rows, col_width).astype(jnp.bfloat16)


def solution(mesh):
    return jax.shard_map(
        per_device,
        mesh=mesh,
        in_specs=(P("seq", "tp"), P("seq", "tp"), P("seq", "tp"), P("tp"), P("tp")),
        out_specs=P("seq", "tp"),
        check_vma=False,
    )
```

profile of v0, /device:TPU:1, one launch (start us, length us, event | category | flops | bytes accessed | tf_op | source)
XLA Modules:
  0.0 272.2 jit_solution(13587932679675128772)
XLA Ops:
  1.2 8.8 %collective-permute-start.3 = (bf16[128,1280]{0,1:T(8,128)(2,1)S(1)}, bf16[128,1280]{0,1:T(8,128)(2,1)S(1)}, u32[]{:S(2)}, u32[]{:S(2)}) collective-permute-start(bf16[128,1280]{0,1:T(8,128)(2,1)S(1)} %copy.30), channel_id=1, source_target_pairs={{0,4},{4,0},{8,12},{12,8},{16,20},{20,16},{24,28},{28,24},{32,36},... | collective-permute-start | bytes 983048 | tf_op jit(solution)/shard_map/ppermute | solution.py:15
  11.6 6.9 %all-reduce = (f32[128]{0:T(128)S(1)}, f32[128]{0:T(128)S(1)}) all-reduce(f32[128]{0:T(128)S(1)} %get-tuple-element.57, f32[128]{0:T(128)S(1)} %get-tuple-element.58), channel_id=1, replica_groups=mesh['seq'=128,'tp'=4] {'tp'}, use_global_device_ids=true, to_apply=%region_1.0 | all-reduce | flops 256 | bytes 2048 | tf_op jit(solution)/shard_map/psum | solution.py:59
  18.8 3.7 %collective-permute-start = (bf16[128,1280]{0,1:T(8,128)(2,1)S(1)}, bf16[128,1280]{0,1:T(8,128)(2,1)}, u32[]{:S(2)}, u32[]{:S(2)}) collective-permute-start(bf16[128,1280]{0,1:T(8,128)(2,1)S(1)} %fusion.23), channel_id=1, source_target_pairs={{0,4},{4,0},{8,12},{12,8},{16,20},{20,16},{24,28},{28,24},{32,36},... | collective-permute-start | bytes 983048 | tf_op jit(solution)/shard_map/ppermute | solution.py:15
  23.7 13.2 %all-to-all-start.1 = ((bf16[1,128,10,128]{3,2,0,1:T(8,128)(2,1)}), bf16[1,128,10,128]{3,2,0,1:T(8,128)(2,1)S(1)}, u32[]{:S(2)}, u32[]{:S(2)}) async-start(bf16[1,128,10,128]{3,2,0,1:T(8,128)(2,1)} %copy.40), calls=%async_computation.1 | async-start | bytes 1048576 | tf_op jit(solution)/shard_map/all_to_all | solution.py:87
  38.4 16.5 %all-to-all-done.1 = bf16[1,128,10,128]{3,2,0,1:T(8,128)(2,1)S(1)} async-done(((bf16[1,128,10,128]{3,2,0,1:T(8,128)(2,1)}), bf16[1,128,10,128]{3,2,0,1:T(8,128)(2,1)S(1)}, u32[]{:S(2)}, u32[]{:S(2)}) %all-to-all-start.1) | async-done | bytes 327712 | tf_op jit(solution)/shard_map/all_to_all | solution.py:87
  54.9 7.6 %all-to-all-start = ((bf16[1,128,10,128]{3,2,0,1:T(8,128)(2,1)}), bf16[1,128,10,128]{3,2,0,1:T(8,128)(2,1)}, u32[]{:S(2)}, u32[]{:S(2)}) async-start(bf16[1,128,10,128]{3,2,0,1:T(8,128)(2,1)} %copy.38), calls=%async_computation | async-start | bytes 1048576 | tf_op jit(solution)/shard_map/all_to_all | solution.py:86
  62.8 3.3 %collective-permute-start.4 = (bf16[256,1280]{0,1:T(8,128)(2,1)S(1)}, bf16[256,1280]{0,1:T(8,128)(2,1)S(1)}, u32[]{:S(2)}, u32[]{:S(2)}) collective-permute-start(bf16[256,1280]{0,1:T(8,128)(2,1)S(1)} %maximum_select_fusion.9), channel_id=1, source_target_pairs={{0,8},{4,12},{8,0},{12,4},{16,24},{20,28},{24,16},{28,20},{32,40},... | collective-permute-start | bytes 1966088 | tf_op jit(solution)/shard_map/ppermute | solution.py:15
  67.4 2.0 collective-permute-start.1
  70.6 9.6 %all-to-all-done = bf16[1,128,10,128]{3,2,0,1:T(8,128)(2,1)} async-done(((bf16[1,128,10,128]{3,2,0,1:T(8,128)(2,1)}), bf16[1,128,10,128]{3,2,0,1:T(8,128)(2,1)}, u32[]{:S(2)}, u32[]{:S(2)}) %all-to-all-start) | async-done | bytes 327712 | tf_op jit(solution)/shard_map/all_to_all | solution.py:86
  80.2 7.7 %all-to-all-start.2 = ((bf16[1,128,10,128]{3,2,0,1:T(8,128)(2,1)}), bf16[1,128,10,128]{3,2,0,1:T(8,128)(2,1)}, u32[]{:S(2)}, u32[]{:S(2)}) async-start(bf16[1,128,10,128]{3,2,0,1:T(8,128)(2,1)} %copy.45), calls=%async_computation.2 | async-start | bytes 1048576 | tf_op jit(solution)/shard_map/all_to_all | solution.py:88
  87.9 2.6 convolution_multiply_fusion.1
  91.9 4.3 %collective-permute-start.5 = (bf16[512,1280]{0,1:T(8,128)(2,1)}, bf16[512,1280]{0,1:T(8,128)(2,1)}, u32[]{:S(2)}, u32[]{:S(2)}) collective-permute-start(bf16[512,1280]{0,1:T(8,128)(2,1)} %maximum_select_fusion.5), channel_id=1, source_target_pairs={{0,16},{4,20},{8,24},{12,28},{16,0},{20,4},{24,8},{28,12},{32,48},... | collective-permute-start | bytes 3932168 | tf_op jit(solution)/shard_map/ppermute | solution.py:15
  96.2 29.2 %collective-permute-done.1 = bf16[256,1280]{0,1:T(8,128)(2,1)S(1)} collective-permute-done((bf16[256,1280]{0,1:T(8,128)(2,1)S(1)}, bf16[256,1280]{0,1:T(8,128)(2,1)S(1)}, u32[]{:S(2)}, u32[]{:S(2)}) %collective-permute-start.1) | collective-permute-done | bytes 655392 | tf_op jit(solution)/shard_map/ppermute | solution.py:15
  126.8 2.2 collective-permute-start.2
  129.0 1.7 fusion.36
  130.7 3.1 %all-to-all-done.2 = bf16[1,128,10,128]{3,2,0,1:T(8,128)(2,1)} async-done(((bf16[1,128,10,128]{3,2,0,1:T(8,128)(2,1)}), bf16[1,128,10,128]{3,2,0,1:T(8,128)(2,1)}, u32[]{:S(2)}, u32[]{:S(2)}) %all-to-all-start.2) | async-done | bytes 327712 | tf_op jit(solution)/shard_map/all_to_all | solution.py:88
  136.6 10.1 %all-to-all-start.3 = ((bf16[128,1,10,128]{3,2,1,0:T(8,128)(2,1)}), bf16[128,1,10,128]{3,2,1,0:T(8,128)(2,1)}, u32[]{:S(2)}, u32[]{:S(2)}) async-start(bf16[128,1,10,128]{3,2,1,0:T(8,128)(2,1)} %copy.50), calls=%async_computation.3 | async-start | bytes 1048576 | tf_op jit(solution)/shard_map/all_to_all | solution.py:90
  150.1 79.4 %all-to-all-done.3 = bf16[128,1,10,128]{3,2,1,0:T(8,128)(2,1)} async-done(((bf16[128,1,10,128]{3,2,1,0:T(8,128)(2,1)}), bf16[128,1,10,128]{3,2,1,0:T(8,128)(2,1)}, u32[]{:S(2)}, u32[]{:S(2)}) %all-to-all-start.3) | async-done | bytes 327712 | tf_op jit(solution)/shard_map/all_to_all | solution.py:90
  229.4 2.1 copy.51
  231.5 3.6 %fusion.14 = bf16[10,1024,128]{1,2,0:T(8,128)(2,1)} fusion(bf16[512,10,128]{0,2,1:T(8,128)(2,1)} %bitcast.14, bf16[512,10,128]{0,2,1:T(8,128)(2,1)S(1)} %maximum_select_fusion.4, pred[]{:T(512)S(6)} %eq.9), kind=kLoop, calls=%fused_computation.20 | loop fusion | flops 11796480 | bytes 5242881 | tf_op jit(solution)/shard_map/transpose | solution.py:80
  235.1 2.5 fusion.13
  237.6 32.4 %while.10 = (s32[]{:T(128)}, f32[10,128,128]{1,2,0:T(8,128)}, bf16[10,128,128]{1,2,0:T(8,128)(2,1)}, bf16[10,1024,128]{1,2,0:T(8,128)(2,1)S(1)}, bf16[10,1024,128]{1,2,0:T(8,128)(2,1)}, /*index=5*/s32[]{:T(128)}) while((s32[]{:T(128)}, f32[10,128,128]{1,2,0:T(8,128)}, bf16[10,128,128]{1,2,0:T(8,128)(2,1)}, ...), condition=%wide.region_7.8_spmd, body=%wide.region_4.7_spmd.sunk | while | flops 68026112 | bytes 2200133 | solution.py:81
  239.0 1.9 fusion.49
  242.2 1.9 fusion.49
  245.4 1.9 fusion.49
  248.7 1.9 fusion.49
  251.9 1.9 fusion.49
  255.1 1.9 fusion.49
  258.4 1.9 fusion.49
  261.6 1.9 fusion.49
  264.9 1.9 fusion.49
  268.1 1.9 fusion.49
  (70 shorter events, 32.5 us)
Async XLA Ops:
  0.0 11.2 %copy-start.7 = (bf16[128,1280]{1,0:T(8,128)(2,1)S(1)}, bf16[128,1280]{1,0:T(8,128)(2,1)}, u32[]{:S(2)}) copy-start(bf16[128,1280]{1,0:T(8,128)(2,1)} %param.8) | copy-start | bytes 983044
  0.0 18.5 %copy-start.8 = (f32[1280]{0:T(1024)S(1)}, f32[1280]{0:T(1024)}, u32[]{:S(2)}) copy-start(f32[1280]{0:T(1024)} %param.11) | copy-start | bytes 15364
  1.2 61.3 %collective-permute-start.3 = (bf16[128,1280]{0,1:T(8,128)(2,1)S(1)}, bf16[128,1280]{0,1:T(8,128)(2,1)S(1)}, u32[]{:S(2)}, u32[]{:S(2)}) collective-permute-start(bf16[128,1280]{0,1:T(8,128)(2,1)S(1)} %copy.30), channel_id=1, source_target_pairs={{0,4},{4,0},{8,12},{12,8},{16,20},{20,16},{24,28},{28,24},{32,36},... | collective-permute-start | bytes 983048 | tf_op jit(solution)/shard_map/ppermute | solution.py:15
  11.6 25.3 %copy-start.9 = (f32[1280]{0:T(1024)S(1)}, f32[1280]{0:T(1024)}, u32[]{:S(2)}) copy-start(f32[1280]{0:T(1024)} %param.10) | copy-start | bytes 15364
  18.8 47.3 %collective-permute-start = (bf16[128,1280]{0,1:T(8,128)(2,1)S(1)}, bf16[128,1280]{0,1:T(8,128)(2,1)}, u32[]{:S(2)}, u32[]{:S(2)}) collective-permute-start(bf16[128,1280]{0,1:T(8,128)(2,1)S(1)} %fusion.23), channel_id=1, source_target_pairs={{0,4},{4,0},{8,12},{12,8},{16,20},{20,16},{24,28},{28,24},{32,36},... | collective-permute-start | bytes 983048 | tf_op jit(solution)/shard_map/ppermute | solution.py:15
  23.7 31.2 %all-to-all-start.1 = ((bf16[1,128,10,128]{3,2,0,1:T(8,128)(2,1)}), bf16[1,128,10,128]{3,2,0,1:T(8,128)(2,1)S(1)}, u32[]{:S(2)}, u32[]{:S(2)}) async-start(bf16[1,128,10,128]{3,2,0,1:T(8,128)(2,1)} %copy.40), calls=%async_computation.1 | async-start | bytes 1048576 | tf_op jit(solution)/shard_map/all_to_all | solution.py:87
  37.1 25.4 %copy-start.1 = (bf16[128,1280]{0,1:T(8,128)(2,1)}, bf16[128,1280]{0,1:T(8,128)(2,1)S(1)}, u32[]{:S(2)}) copy-start(bf16[128,1280]{0,1:T(8,128)(2,1)S(1)} %fusion.20) | copy-start | bytes 983044
  54.9 11.3 %copy-start.2 = (bf16[1,128,10,128]{3,2,0,1:T(8,128)(2,1)}, bf16[1,128,10,128]{3,2,0,1:T(8,128)(2,1)S(1)}, u32[]{:S(2)}) copy-start(bf16[1,128,10,128]{3,2,0,1:T(8,128)(2,1)S(1)} %all-to-all-done.1) | copy-start | bytes 983044
  54.9 25.3 %all-to-all-start = ((bf16[1,128,10,128]{3,2,0,1:T(8,128)(2,1)}), bf16[1,128,10,128]{3,2,0,1:T(8,128)(2,1)}, u32[]{:S(2)}, u32[]{:S(2)}) async-start(bf16[1,128,10,128]{3,2,0,1:T(8,128)(2,1)} %copy.38), calls=%async_computation | async-start | bytes 1048576 | tf_op jit(solution)/shard_map/all_to_all | solution.py:86
  62.6 3.6 %copy-start.4 = (bf16[128,1280]{0,1:T(8,128)(2,1)}, bf16[128,1280]{0,1:T(8,128)(2,1)S(1)}, u32[]{:S(2)}) copy-start(bf16[128,1280]{0,1:T(8,128)(2,1)S(1)} %collective-permute-done.3) | copy-start | bytes 983044
  62.8 27.7 %collective-permute-start.4 = (bf16[256,1280]{0,1:T(8,128)(2,1)S(1)}, bf16[256,1280]{0,1:T(8,128)(2,1)S(1)}, u32[]{:S(2)}, u32[]{:S(2)}) collective-permute-start(bf16[256,1280]{0,1:T(8,128)(2,1)S(1)} %maximum_select_fusion.9), channel_id=1, source_target_pairs={{0,8},{4,12},{8,0},{12,4},{16,24},{20,28},{24,16},{28,20},{32,40},... | collective-permute-start | bytes 1966088 | tf_op jit(solution)/shard_map/ppermute | solution.py:15
  67.4 58.0 %collective-permute-start.1 = (bf16[256,1280]{0,1:T(8,128)(2,1)S(1)}, bf16[256,1280]{0,1:T(8,128)(2,1)S(1)}, u32[]{:S(2)}, u32[]{:S(2)}) collective-permute-start(bf16[256,1280]{0,1:T(8,128)(2,1)S(1)} %maximum_select_fusion.7), channel_id=1, source_target_pairs={{0,8},{4,12},{8,0},{12,4},{16,24},{20,28},{24,16},{28,20},{32,40},... | collective-permute-start | bytes 1966088 | tf_op jit(solution)/shard_map/ppermute | solution.py:15
  80.2 53.6 %all-to-all-start.2 = ((bf16[1,128,10,128]{3,2,0,1:T(8,128)(2,1)}), bf16[1,128,10,128]{3,2,0,1:T(8,128)(2,1)}, u32[]{:S(2)}, u32[]{:S(2)}) async-start(bf16[1,128,10,128]{3,2,0,1:T(8,128)(2,1)} %copy.45), calls=%async_computation.2 | async-start | bytes 1048576 | tf_op jit(solution)/shard_map/all_to_all | solution.py:88
  91.9 37.2 %copy-start.3 = (bf16[1,128,10,128]{3,2,0,1:T(8,128)(2,1)S(1)}, bf16[1,128,10,128]{3,2,0,1:T(8,128)(2,1)}, u32[]{:S(2)}) copy-start(bf16[1,128,10,128]{3,2,0,1:T(8,128)(2,1)} %copy-done.2) | copy-start | bytes 983044
  91.9 139.7 %collective-permute-start.5 = (bf16[512,1280]{0,1:T(8,128)(2,1)}, bf16[512,1280]{0,1:T(8,128)(2,1)}, u32[]{:S(2)}, u32[]{:S(2)}) collective-permute-start(bf16[512,1280]{0,1:T(8,128)(2,1)} %maximum_select_fusion.5), channel_id=1, source_target_pairs={{0,16},{4,20},{8,24},{12,28},{16,0},{20,4},{24,8},{28,12},{32,48},... | collective-permute-start | bytes 3932168 | tf_op jit(solution)/shard_map/ppermute | solution.py:15
  126.8 7.1 %copy-start.6 = (f32[8,10,16,16]{2,3,1,0:T(8,128)S(1)}, f32[8,10,16,16]{2,3,1,0:T(8,128)}, u32[]{:S(2)}) copy-start(f32[8,10,16,16]{2,3,1,0:T(8,128)} %convolution_multiply_fusion.1) | copy-start | bytes 245764
  126.8 108.3 %collective-permute-start.2 = (bf16[512,1280]{0,1:T(8,128)(2,1)}, bf16[512,1280]{0,1:T(8,128)(2,1)}, u32[]{:S(2)}, u32[]{:S(2)}) collective-permute-start(bf16[512,1280]{0,1:T(8,128)(2,1)} %maximum_select_fusion.3), channel_id=1, source_target_pairs={{0,16},{4,20},{8,24},{12,28},{16,0},{20,4},{24,8},{28,12},{32,48},... | collective-permute-start | bytes 3932168 | tf_op jit(solution)/shard_map/ppermute | solution.py:15
  135.4 11.4 %copy-start.5 = (bf16[128,1280]{0,1:T(8,128)(2,1)S(1)}, bf16[128,1280]{0,1:T(8,128)(2,1)}, u32[]{:S(2)}) copy-start(bf16[128,1280]{0,1:T(8,128)(2,1)} %copy-done.4) | copy-start | bytes 983044
  136.6 92.9 %all-to-all-start.3 = ((bf16[128,1,10,128]{3,2,1,0:T(8,128)(2,1)}), bf16[128,1,10,128]{3,2,1,0:T(8,128)(2,1)}, u32[]{:S(2)}, u32[]{:S(2)}) async-start(bf16[128,1,10,128]{3,2,1,0:T(8,128)(2,1)} %copy.50), calls=%async_computation.3 | async-start | bytes 1048576 | tf_op jit(solution)/shard_map/all_to_all | solution.py:90
  231.5 3.6 %copy-start = (bf16[512,10,128]{0,2,1:T(8,128)(2,1)S(1)}, bf16[512,10,128]{0,2,1:T(8,128)(2,1)}, u32[]{:S(2)}) copy-start(bf16[512,10,128]{0,2,1:T(8,128)(2,1)} %maximum_select_fusion.2) | copy-start | bytes 3932164
where the time goes:
time: 274 us; the launch traced here: 272 us
  waiting for transfers between devices  138 us (50%)
  starting transfers between devices  63 us (23%)
  matrix products  35.8 us (13%)
  other arithmetic  17.9 us (7%)
  local copies, waits for them, and re-layouts  10.4 us (4%)
  blocking collectives  6.91 us (3%)
    all_to_all x1, waiting for transfers between devices, per_device(): lax.all_to_all(temporal_mix(switched, group), 'seq', split_axis=0, concat...  79.4 us
    ppermute x6, waiting for transfers between devices, swapped(): return lax.ppermute(value, axis, pairs)  29.2 us
    ppermute x6, starting transfers between devices, swapped(): return lax.ppermute(value, axis, pairs)  24.3 us
    dot_general x10, matrix products, one_head(): return jnp.dot(weights, v_head, preferred_element_type=jnp.float32)  19.2 us
    all_to_all x1, waiting for transfers between devices, per_device(): lax.all_to_all(k_four, 'seq', split_axis=1, concat_axis=0, tiled=True)  16.5 us
    all_to_all x1, starting transfers between devices, per_device(): lax.all_to_all(k_four, 'seq', split_axis=1, concat_axis=0, tiled=True)  13.2 us
    dot_general x10, matrix products, one_head(): jnp.dot(q_head, k_head.T, preferred_element_type=jnp.float32)  10.9 us
    all_to_all x1, starting transfers between devices, per_device(): lax.all_to_all(temporal_mix(switched, group), 'seq', split_axis=0, concat...  10.1 us
  transfers between devices with their start and end apart: 10, of which 5 were waited for; matrix products, arithmetic and copies ran while one was open for 9% of the time, Pallas kernels for 0%

commit v1 on v0

v1 whole, which is shorter than its diff:
```python
import math

import jax
import jax.numpy as jnp
from jax import lax
from jax.experimental import pallas as pl
from jax.experimental.pallas import tpu as pltpu
from jax.sharding import Mesh, PartitionSpec as P

D = 5120
HEAD = 128
EPS = 1e-06
SCALE = 1.0 / math.sqrt(HEAD)
SEQ = ("x", "yl", "zh", "zl", "c")
FRAME = ("x", "yl", "zh")


def contract_last(a, b):
    return lax.dot_general(a, b, (((1,), (1,)), ((), ())), preferred_element_type=jnp.float32)


def softmax_times(scores, v):
    top = jnp.max(scores, axis=-1, keepdims=True)
    raised = jnp.exp((scores - top) * SCALE)
    total = jnp.sum(raised, axis=-1, keepdims=True)
    out = jnp.dot(raised.astype(jnp.bfloat16), v, preferred_element_type=jnp.float32)
    return out / total


def normed(x, stat, gain):
    scale = lax.rsqrt(stat / D + EPS)
    return (x.astype(jnp.float32) * scale * gain).astype(jnp.bfloat16)


def spatial_kernel(q_ref, qs_ref, ks_ref, qg_ref, kg_ref, b0, b1, b2, b3, out_ref, k_all, v_all):
    n = q_ref.shape[0]
    for i, blk in enumerate((b0, b1, b2, b3)):
        rows = pl.ds(i * n, n)
        k_all[rows, :] = normed(blk[pl.ds(0, n), :], ks_ref[rows, :], kg_ref[...])
        v_all[rows, :] = blk[pl.ds(n, n), :]
    q = normed(q_ref[...], qs_ref[...], qg_ref[...])
    out_ref[...] = softmax_times(contract_last(q, k_all[...]), v_all[...])


def spatial(q, qs, ks, qg, kg, blocks):
    n, width = q.shape
    heads = width // HEAD
    col = lambda rows: pl.BlockSpec((rows, HEAD), lambda h: (0, h))
    whole = lambda rows: pl.BlockSpec((rows, 1), lambda h: (0, 0))
    return pl.pallas_call(
        spatial_kernel,
        grid=(heads,),
        out_shape=jax.ShapeDtypeStruct((n, width), jnp.float32),
        in_specs=[col(n), whole(n), whole(4 * n), col(1), col(1)] + [col(2 * n)] * 4,
        out_specs=col(n),
        scratch_shapes=[
            pltpu.VMEM((4 * n, HEAD), jnp.bfloat16),
            pltpu.VMEM((4 * n, HEAD), jnp.bfloat16),
        ],
        compiler_params=pltpu.CompilerParams(vmem_limit_bytes=24 << 20),
        cost_estimate=pl.CostEstimate(
            flops=heads * n * n * 4 * HEAD * 4, bytes_accessed=n * width * 22, transcendentals=heads * n * n * 4
        ),
    )(q, qs, ks, qg, kg, *blocks)


def temporal_kernel(q_ref, k_ref, v_ref, out_ref, *, per):
    n = q_ref.shape[0]
    row = lax.broadcasted_iota(jnp.int32, (n, n), 0)
    column = lax.broadcasted_iota(jnp.int32, (n, n), 1)
    same = (row - column) % per == 0
    scores = contract_last(q_ref[...], k_ref[...])
    scores = jnp.where(same, scores, -1e30)
    out_ref[...] = softmax_times(scores, v_ref[...]).astype(jnp.bfloat16)


def temporal(q, k, v, per):
    n, width = q.shape
    heads = width // HEAD
    col = pl.BlockSpec((n, HEAD), lambda h: (0, h))
    return pl.pallas_call(
        lambda *refs: temporal_kernel(*refs, per=per),
        grid=(heads,),
        out_shape=jax.ShapeDtypeStruct((n, width), jnp.bfloat16),
        in_specs=[col] * 3,
        out_specs=col,
        compiler_params=pltpu.CompilerParams(vmem_limit_bytes=24 << 20),
        cost_estimate=pl.CostEstimate(
            flops=heads * n * n * HEAD * 4, bytes_accessed=n * width * 8, transcendentals=heads * n * n
        ),
    )(q, k, v)


def per_device(queries, keys, values, query_gain, key_gain):
    tok, width = queries.shape
    half = width // 2
    zl, core = lax.axis_index("zl"), lax.axis_index("c")
    frames = lax.axis_size(FRAME)

    def mine(a):
        return lax.dynamic_slice_in_dim(a, core * half, half, a.ndim - 1)

    def other(a):
        return lax.dynamic_slice_in_dim(a, (1 - core) * half, half, a.ndim - 1)

    swap = [(0, 1), (1, 0)]
    sent = jnp.concatenate([other(keys), other(values), other(queries)], axis=0)
    got = lax.ppermute(sent, "c", swap)
    own_kv = jnp.concatenate([mine(keys), got[:tok], mine(values), got[tok : 2 * tok]], axis=0)
    own_q = jnp.concatenate([mine(queries), got[2 * tok :]], axis=0)

    up = [(i, i + 1) for i in range(3)]
    down = [(i + 1, i) for i in range(3)]
    plus1 = lax.ppermute(own_kv, "zl", up)
    minus1 = lax.ppermute(own_kv, "zl", down)
    plus2 = lax.ppermute(plus1, "zl", up[1:])
    minus2 = lax.ppermute(minus1, "zl", down[:-1])
    plus3 = lax.ppermute(plus2, "zl", up[2:])
    minus3 = lax.ppermute(minus2, "zl", down[:1])

    part = jnp.stack(
        [
            jnp.sum(jnp.square(queries.astype(jnp.float32)), axis=1),
            jnp.sum(jnp.square(keys.astype(jnp.float32)), axis=1),
        ]
    )
    place = lax.broadcasted_iota(jnp.int32, (8, 1, 1), 0) == zl * 2 + core
    stats = lax.psum(jnp.where(place, part[None], 0.0), ("tp", "zl", "c"))
    stat_of = lambda z, c: lax.dynamic_index_in_dim(stats, z * 2 + c, 0, keepdims=False)
    own_stat, twin_stat = stat_of(zl, core), stat_of(zl, 1 - core)
    q_norm = normed(queries, own_stat[0][:, None], query_gain[None, :])
    k_norm = normed(keys, own_stat[1][:, None], key_gain[None, :])

    def to_positions(a):
        return lax.all_to_all(a.reshape(frames, tok // frames, width), FRAME, 0, 0, tiled=True)

    tq, tk, tv = (to_positions(a).reshape(tok, width) for a in (q_norm, k_norm, values))
    t_out = temporal(tq, tk, tv, tok // frames)
    t_back = to_positions(t_out).reshape(tok, width)

    blocks = [
        own_kv,
        jnp.where(zl >= 1, plus1, minus3),
        jnp.where(zl >= 2, plus2, minus2),
        jnp.where(zl >= 3, plus3, minus1),
    ]
    q_stat = jnp.concatenate([own_stat[0], twin_stat[0]])[:, None]
    k_stat = jnp.concatenate(
        [stat_of((zl - j) % 4, c)[1] for j in range(4) for c in (core, 1 - core)]
    )[:, None]
    s_out = spatial(own_q, q_stat, k_stat, mine(query_gain)[None], mine(key_gain)[None], blocks)
    s_got = lax.ppermute(s_out[tok:], "c", swap)
    s_mine = s_out[:tok]
    s_all = jnp.where(
        core == 0,
        jnp.concatenate([s_mine, s_got], axis=1),
        jnp.concatenate([s_got, s_mine], axis=1),
    )
    return (s_all + t_back.astype(jnp.float32)).astype(jnp.bfloat16)


def solution(mesh):
    axes = SEQ + ("tp",)
    split = Mesh(mesh.devices.reshape(4, 2, 2, 4, 2, 4), axes)
    return jax.shard_map(
        per_device,
        mesh=split,
        in_specs=(P(SEQ, "tp"), P(SEQ, "tp"), P(SEQ, "tp"), P("tp"), P("tp")),
        out_specs=P(SEQ, "tp"),
        check_vma=False,
    )
```

time: 274 us -> 178 us (0.65)
  waiting for transfers between devices: 138 us -> 24.2 us
  blocking collectives: 6.91 us -> 74.9 us
  matrix products: 35.8 us -> 0 us
  Pallas kernels: 0 us -> 10.6 us
  other arithmetic: 17.9 us -> 7.54 us
  starting transfers between devices: 63 us -> 55.7 us
  local copies, waits for them, and re-layouts: 10.4 us -> 3.53 us
    all_to_all x4, waiting for transfers between devices: 109 us -> 14.6 us  [to_positions(): lax.all_to_all(a.reshape(frames, tok // frames, width), FRAME, 0, 0, tile...]
    psum x1, blocking collectives: 6.91 us -> 74.9 us  [per_device(): stats = lax.psum(jnp.where(place, part[None], 0.0), ('tp', 'zl', 'c'))]
    dot_general x22 -> x0, matrix products: 34.1 us -> none  [the longest x10 19.2 us: one_head(): return jnp.dot(weights, v_head, preferred_element_type=jnp.float32)]
    ppermute x6 -> x8, waiting for transfers between devices: 29.2 us -> 9.62 us  [the longest x1 8.39 us: per_device(): minus2 = lax.ppermute(minus1, 'zl', down[:-1])]
    all_to_all x4, starting transfers between devices: 38.7 us -> 27.3 us  [to_positions(): lax.all_to_all(a.reshape(frames, tok // frames, width), FRAME, 0, 0, tile...]
    pallas_call x0 -> x2, Pallas kernels: none -> 10.6 us  [the longest x1 5.43 us: temporal(): pl.pallas_call(lambda *refs: temporal_kernel(*refs, per=per), grid=(heads...]
    transpose x2 -> x0, other arithmetic: 6.09 us -> none  [the longest x1 3.6 us: per_device(): frame_v.reshape(frame_len, head_count, HEAD_DIM).transpose(1, 0, 2)]
    reshape x4 -> x0, local copies, waits for them, and re-layouts: 4.66 us -> none  [the longest x1 1.21 us: per_device(): v_four = values.reshape(1, tok_rows, head_count, HEAD_DIM)]
  transfers between devices with their start and end apart: 10 -> 12, of which waited for: 5 -> 4; matrix products, arithmetic and copies ran while one was open for 9% -> 5% of each run, Pallas kernels for 0% -> 6%
where the time goes in v1:
time: 178 us; the launch traced here: 177 us
  blocking collectives  74.9 us (42%)
  starting transfers between devices  55.7 us (31%)
  waiting for transfers between devices  24.2 us (14%)
  Pallas kernels  10.6 us (6%)
  other arithmetic  7.54 us (4%)
  local copies, waits for them, and re-layouts  3.53 us (2%)
    psum x1, blocking collectives, per_device(): stats = lax.psum(jnp.where(place, part[None], 0.0), ('tp', 'zl', 'c'))  74.9 us
    all_to_all x4, starting transfers between devices, to_positions(): lax.all_to_all(a.reshape(frames, tok // frames, width), FRAME, 0, 0, tile...  27.3 us
    all_to_all x4, waiting for transfers between devices, to_positions(): lax.all_to_all(a.reshape(frames, tok // frames, width), FRAME, 0, 0, tile...  14.6 us
    ppermute x1, starting transfers between devices, per_device(): s_got = lax.ppermute(s_out[tok:], 'c', swap)  11.3 us
    ppermute x1, starting transfers between devices, per_device(): got = lax.ppermute(sent, 'c', swap)  8.91 us
    ppermute x1, waiting for transfers between devices, per_device(): minus2 = lax.ppermute(minus1, 'zl', down[:-1])  8.39 us
    pallas_call x1, Pallas kernels, temporal(): pl.pallas_call(lambda *refs: temporal_kernel(*refs, per=per), grid=(heads...  5.43 us
    pallas_call x1, Pallas kernels, spatial(): pl.pallas_call(spatial_kernel, grid=(heads,), out_shape=jax.ShapeDtypeStr...  5.21 us
  transfers between devices with their start and end apart: 12, of which 4 were waited for; matrix products, arithmetic and copies ran while one was open for 5% of the time, Pallas kernels for 6%

profile of v1, /device:TPU:1, one launch (start us, length us, event | category | flops | bytes accessed | tf_op | source)
XLA Modules:
  0.0 177.1 jit_solution(9093795862808426777)
XLA Ops:
  0.0 1.1 constant_dynamic-slice_fusion.1
  1.1 1.0 constant_dynamic-slice_fusion
  2.3 8.9 %collective-permute-start = (bf16[384,640]{1,0:T(8,128)(2,1)S(1)}, bf16[384,640]{1,0:T(8,128)(2,1)S(1)}, u32[]{:S(2)}, u32[]{:S(2)}) collective-permute-start(bf16[384,640]{1,0:T(8,128)(2,1)S(1)} %pad_maximum_fusion.1), channel_id=1, source_target_pairs={{0,4},{4,0},{1,5},{5,1},{2,6},{6,2},{3,7},{7,3},{8,12},{12,8},{9,1... | collective-permute-start | bytes 1474568 | tf_op jit(solution)/shard_map/ppermute | solution.py:108
  11.3 0.1 fusion
  11.4 0.1 fusion.3
  11.7 74.9 %psum.7 = f32[8,2,128]{2,1,0:T(2,128)S(1)} all-reduce(f32[8,2,128]{2,1,0:T(2,128)S(1)} %broadcast_select_fusion.3), channel_id=1, replica_groups=mesh['x'=4,'yl'=2,'zh'=2,'zl'=4,'c'=2,'tp'=4] {'tp','zl','c'}, use_global_device_ids=true, to_apply=%region_2.3 | all-reduce | flops 2048 | bytes 16384 | tf_op jit(solution)/shard_map/psum | solution.py:128
  86.7 0.9 fusion.8
  87.6 8.2 %all-to-all-start.1 = ((bf16[16,8,1280]{2,1,0:T(8,128)(2,1)}), bf16[16,8,1280]{2,1,0:T(8,128)(2,1)S(1)}, u32[]{:S(2)}, u32[]{:S(2)}) async-start(bf16[16,8,1280]{2,1,0:T(8,128)(2,1)} %fusion.8), calls=%async_computation.1 | async-start | bytes 655360 | tf_op jit(solution)/shard_map/all_to_all | solution.py:135
  95.9 0.9 fusion.9
  96.7 0.7 fusion.11
  97.5 1.3 collective-permute-start.1
  98.8 1.3 collective-permute-start.2
  100.2 6.6 %all-to-all-done.1 = bf16[16,8,1280]{2,1,0:T(8,128)(2,1)S(1)} async-done(((bf16[16,8,1280]{2,1,0:T(8,128)(2,1)}), bf16[16,8,1280]{2,1,0:T(8,128)(2,1)S(1)}, u32[]{:S(2)}, u32[]{:S(2)}) %all-to-all-start.1) | async-done | bytes 327712 | tf_op jit(solution)/shard_map/all_to_all | solution.py:135
  106.8 4.1 %all-to-all-start = ((bf16[16,8,1280]{2,1,0:T(8,128)(2,1)}), bf16[16,8,1280]{2,1,0:T(8,128)(2,1)S(1)}, u32[]{:S(2)}, u32[]{:S(2)}) async-start(bf16[16,8,1280]{2,1,0:T(8,128)(2,1)} %fusion.9), calls=%async_computation | async-start | bytes 655360 | tf_op jit(solution)/shard_map/all_to_all | solution.py:135
  110.9 1.5 collective-permute-start.5
  112.5 1.3 collective-permute-start.3
  114.0 7.9 %all-to-all-done = bf16[16,8,1280]{2,1,0:T(8,128)(2,1)S(1)} async-done(((bf16[16,8,1280]{2,1,0:T(8,128)(2,1)}), bf16[16,8,1280]{2,1,0:T(8,128)(2,1)S(1)}, u32[]{:S(2)}, u32[]{:S(2)}) %all-to-all-start) | async-done | bytes 327712 | tf_op jit(solution)/shard_map/all_to_all | solution.py:135
  121.9 5.0 %all-to-all-start.2 = ((bf16[16,8,1280]{2,1,0:T(8,128)(2,1)}), bf16[16,8,1280]{2,1,0:T(8,128)(2,1)S(1)}, u32[]{:S(2)}, u32[]{:S(2)}) async-start(bf16[16,8,1280]{2,1,0:T(8,128)(2,1)} %bitcast.19), calls=%async_computation.2 | async-start | bytes 655360 | tf_op jit(solution)/shard_map/all_to_all | solution.py:135
  127.0 1.5 collective-permute-start.6
  128.5 0.2 copy.7.ks_ref
  128.9 8.4 %collective-permute-done.3 = bf16[512,640]{1,0:T(8,128)(2,1)} collective-permute-done((bf16[512,640]{1,0:T(8,128)(2,1)}, bf16[512,640]{1,0:T(8,128)(2,1)}, u32[]{:S(2)}, u32[]{:S(2)}) %collective-permute-start.3) | collective-permute-done | bytes 655392 | tf_op jit(solution)/shard_map/ppermute | solution.py:117
  137.3 1.3 collective-permute-start.4
  138.6 0.9 pad_maximum_fusion.2.q_ref
  139.6 5.4 %shard_map.56 = bf16[128,1280]{1,0:T(8,128)(2,1)} custom-call(bf16[128,1280]{1,0:T(8,128)(2,1)S(1)} %bitcast.41, bf16[128,1280]{1,0:T(8,128)(2,1)S(1)} %bitcast.40, bf16[128,1280]{1,0:T(8,128)(2,1)S(1)} %bitcast.42), custom_call_target="tpu_custom_call" | custom-call | flops 83886080 | bytes 1310720 | tf_op jit(solution)/shard_map/pallas_call | solution.py:81
  145.0 9.9 %all-to-all-start.3 = ((bf16[16,8,1280]{2,1,0:T(8,128)(2,1)}), bf16[16,8,1280]{2,1,0:T(8,128)(2,1)S(1)}, u32[]{:S(2)}, u32[]{:S(2)}) async-start(bf16[16,8,1280]{2,1,0:T(8,128)(2,1)} %bitcast.21), calls=%async_computation.3 | async-start | bytes 655360 | tf_op jit(solution)/shard_map/all_to_all | solution.py:135
  154.9 1.2 broadcast_select_fusion.1.b2
  156.1 1.2 broadcast_select_fusion.b3
  157.3 1.2 broadcast_select_fusion.2.b1
  158.5 5.2 %shard_map.55 = f32[256,640]{1,0:T(8,128)S(1)} custom-call(bf16[256,640]{1,0:T(8,128)(2,1)S(1)} %pad_maximum_fusion.2.q_ref, f32[256,1]{1,0:T(8,128)S(1)} %copy.6.qs_ref, f32[1024,1]{1,0:T(8,128)S(1)} %copy.7.ks_ref, f32[1,640]{1,0:T(1,128)S(1)} %broadcast_in_dim.40.qg_ref, f32[1,640]{1,0:T(1,128)S(1)} %broadcast_in_dim.41.kg_ref, ...), custom_call_target="tpu_custom_call" | custom-call | flops 671088640 | bytes 3604480 | tf_op jit(solution)/shard_map/pallas_call | solution.py:50
  163.7 11.3 %collective-permute-start.7 = (f32[128,640]{1,0:T(8,128)S(1)}, f32[128,640]{1,0:T(8,128)S(1)}, u32[]{:S(2)}, u32[]{:S(2)}) collective-permute-start(f32[128,640]{1,0:T(8,128)S(1)} %get-tuple-element.6), channel_id=1, source_target_pairs={{0,4},{4,0},{1,5},{5,1},{2,6},{6,2},{3,7},{7,3},{8,12},{12,8},{9,1... | collective-permute-start | bytes 983048 | tf_op jit(solution)/shard_map/ppermute | solution.py:152
  175.1 1.2 collective-permute-done.7
  176.3 0.8 fusion.7
  (41 shorter events, 0.7 us)
Async XLA Ops:
  0.0 2.1 %copy-start.1 = (bf16[128,1280]{1,0:T(8,128)(2,1)S(1)}, bf16[128,1280]{1,0:T(8,128)(2,1)}, u32[]{:S(2)}) copy-start(bf16[128,1280]{1,0:T(8,128)(2,1)} %param.5) | copy-start | bytes 983044
  2.2 9.3 %copy-start = (bf16[128,1280]{1,0:T(8,128)(2,1)S(1)}, bf16[128,1280]{1,0:T(8,128)(2,1)}, u32[]{:S(2)}) copy-start(bf16[128,1280]{1,0:T(8,128)(2,1)} %param.6) | copy-start | bytes 983044
  2.2 84.5 %copy-start.3 = (f32[1280]{0:T(1024)S(1)}, f32[1280]{0:T(1024)}, u32[]{:S(2)}) copy-start(f32[1280]{0:T(1024)} %param.9) | copy-start | bytes 15364
  2.3 94.5 %collective-permute-start = (bf16[384,640]{1,0:T(8,128)(2,1)S(1)}, bf16[384,640]{1,0:T(8,128)(2,1)S(1)}, u32[]{:S(2)}, u32[]{:S(2)}) collective-permute-start(bf16[384,640]{1,0:T(8,128)(2,1)S(1)} %pad_maximum_fusion.1), channel_id=1, source_target_pairs={{0,4},{4,0},{1,5},{5,1},{2,6},{6,2},{3,7},{7,3},{8,12},{12,8},{9,1... | collective-permute-start | bytes 1474568 | tf_op jit(solution)/shard_map/ppermute | solution.py:108
  86.7 9.1 %copy-start.2 = (f32[1280]{0:T(1024)S(1)}, f32[1280]{0:T(1024)}, u32[]{:S(2)}) copy-start(f32[1280]{0:T(1024)} %param.8) | copy-start | bytes 15364
  87.6 19.1 %all-to-all-start.1 = ((bf16[16,8,1280]{2,1,0:T(8,128)(2,1)}), bf16[16,8,1280]{2,1,0:T(8,128)(2,1)S(1)}, u32[]{:S(2)}, u32[]{:S(2)}) async-start(bf16[16,8,1280]{2,1,0:T(8,128)(2,1)} %fusion.8), calls=%async_computation.1 | async-start | bytes 655360 | tf_op jit(solution)/shard_map/all_to_all | solution.py:135
  97.5 13.4 %collective-permute-start.1 = (bf16[512,640]{1,0:T(8,128)(2,1)S(1)}, bf16[512,640]{1,0:T(8,128)(2,1)S(1)}, u32[]{:S(2)}, u32[]{:S(2)}) collective-permute-start(bf16[512,640]{1,0:T(8,128)(2,1)S(1)} %pad_maximum_fusion.b0), channel_id=1, source_target_pairs={{0,8},{8,16},{16,24},{1,9},{9,17},{17,25},{2,10},{10,18},{18,26},{... | collective-permute-start | bytes 1966088 | tf_op jit(solution)/shard_map/ppermute | solution.py:114
  98.8 13.6 %collective-permute-start.2 = (bf16[512,640]{1,0:T(8,128)(2,1)S(1)}, bf16[512,640]{1,0:T(8,128)(2,1)}, u32[]{:S(2)}, u32[]{:S(2)}) collective-permute-start(bf16[512,640]{1,0:T(8,128)(2,1)S(1)} %pad_maximum_fusion.b0), channel_id=1, source_target_pairs={{8,0},{16,8},{24,16},{9,1},{17,9},{25,17},{10,2},{18,10},{26,18},{... | collective-permute-start | bytes 1966088 | tf_op jit(solution)/shard_map/ppermute | solution.py:115
  106.8 15.1 %all-to-all-start = ((bf16[16,8,1280]{2,1,0:T(8,128)(2,1)}), bf16[16,8,1280]{2,1,0:T(8,128)(2,1)S(1)}, u32[]{:S(2)}, u32[]{:S(2)}) async-start(bf16[16,8,1280]{2,1,0:T(8,128)(2,1)} %fusion.9), calls=%async_computation | async-start | bytes 655360 | tf_op jit(solution)/shard_map/all_to_all | solution.py:135
  110.9 16.0 %collective-permute-start.5 = (bf16[512,640]{1,0:T(8,128)(2,1)S(1)}, bf16[512,640]{1,0:T(8,128)(2,1)}, u32[]{:S(2)}, u32[]{:S(2)}) collective-permute-start(bf16[512,640]{1,0:T(8,128)(2,1)S(1)} %collective-permute-done.1), channel_id=1, source_target_pairs={{8,16},{16,24},{9,17},{17,25},{10,18},{18,26},{11,19},{19,27},{12,... | collective-permute-start | bytes 1966088 | tf_op jit(solution)/shard_map/ppermute | solution.py:116
  112.5 24.8 %collective-permute-start.3 = (bf16[512,640]{1,0:T(8,128)(2,1)}, bf16[512,640]{1,0:T(8,128)(2,1)}, u32[]{:S(2)}, u32[]{:S(2)}) collective-permute-start(bf16[512,640]{1,0:T(8,128)(2,1)} %collective-permute-done.2), channel_id=1, source_target_pairs={{8,0},{16,8},{9,1},{17,9},{10,2},{18,10},{11,3},{19,11},{12,4},{20... | collective-permute-start | bytes 1966088 | tf_op jit(solution)/shard_map/ppermute | solution.py:117
  121.9 17.6 %all-to-all-start.2 = ((bf16[16,8,1280]{2,1,0:T(8,128)(2,1)}), bf16[16,8,1280]{2,1,0:T(8,128)(2,1)S(1)}, u32[]{:S(2)}, u32[]{:S(2)}) async-start(bf16[16,8,1280]{2,1,0:T(8,128)(2,1)} %bitcast.19), calls=%async_computation.2 | async-start | bytes 655360 | tf_op jit(solution)/shard_map/all_to_all | solution.py:135
  127.0 29.1 %collective-permute-start.6 = (bf16[512,640]{1,0:T(8,128)(2,1)}, bf16[512,640]{1,0:T(8,128)(2,1)}, u32[]{:S(2)}, u32[]{:S(2)}) collective-permute-start(bf16[512,640]{1,0:T(8,128)(2,1)} %collective-permute-done.5), channel_id=1, source_target_pairs={{16,24},{17,25},{18,26},{19,27},{20,28},{21,29},{22,30},{23,31},{4... | collective-permute-start | bytes 1966088 | tf_op jit(solution)/shard_map/ppermute | solution.py:118
  137.3 20.0 %collective-permute-start.4 = (bf16[512,640]{1,0:T(8,128)(2,1)}, bf16[512,640]{1,0:T(8,128)(2,1)}, u32[]{:S(2)}, u32[]{:S(2)}) collective-permute-start(bf16[512,640]{1,0:T(8,128)(2,1)} %collective-permute-done.3), channel_id=1, source_target_pairs={{8,0},{9,1},{10,2},{11,3},{12,4},{13,5},{14,6},{15,7},{40,32},{41,... | collective-permute-start | bytes 1966088 | tf_op jit(solution)/shard_map/ppermute | solution.py:119
  145.0 30.1 %all-to-all-start.3 = ((bf16[16,8,1280]{2,1,0:T(8,128)(2,1)}), bf16[16,8,1280]{2,1,0:T(8,128)(2,1)S(1)}, u32[]{:S(2)}, u32[]{:S(2)}) async-start(bf16[16,8,1280]{2,1,0:T(8,128)(2,1)} %bitcast.21), calls=%async_computation.3 | async-start | bytes 655360 | tf_op jit(solution)/shard_map/all_to_all | solution.py:135
  163.7 12.6 %collective-permute-start.7 = (f32[128,640]{1,0:T(8,128)S(1)}, f32[128,640]{1,0:T(8,128)S(1)}, u32[]{:S(2)}, u32[]{:S(2)}) collective-permute-start(f32[128,640]{1,0:T(8,128)S(1)} %get-tuple-element.6), channel_id=1, source_target_pairs={{0,4},{4,0},{1,5},{5,1},{2,6},{6,2},{3,7},{7,3},{8,12},{12,8},{9,1... | collective-permute-start | bytes 983048 | tf_op jit(solution)/shard_map/ppermute | solution.py:152

commit v2 on v1

v2 whole, which is shorter than its diff:
```python
import math

import jax
import jax.numpy as jnp
from jax import lax
from jax.experimental import pallas as pl
from jax.experimental.pallas import tpu as pltpu
from jax.sharding import Mesh, PartitionSpec as P

D = 5120
HEAD = 128
EPS = 1e-06
SCALE = 1.0 / math.sqrt(HEAD)
SEQ = ("x", "yl", "zh", "zl", "c")
FRAME = ("x", "yl", "zh")


def contract_last(a, b):
    return lax.dot_general(a, b, (((1,), (1,)), ((), ())), preferred_element_type=jnp.float32)


def softmax_times(scores, v):
    top = jnp.max(scores, axis=-1, keepdims=True)
    raised = jnp.exp((scores - top) * SCALE)
    total = jnp.sum(raised, axis=-1, keepdims=True)
    out = jnp.dot(raised.astype(jnp.bfloat16), v, preferred_element_type=jnp.float32)
    return out / total


def normed(x, stat, gain):
    scale = lax.rsqrt(stat / D + EPS)
    return (x.astype(jnp.float32) * scale * gain).astype(jnp.bfloat16)


def spatial_kernel(zl_ref, q_ref, qs_ref, ks_ref, qg_ref, kg_ref, own, p1, m3, p2, m2, p3, m1, out_ref, k_all, v_all):
    n, width = q_ref.shape
    zl = zl_ref[0]
    pairs = ((own, None), (p1, m3), (p2, m2), (p3, m1))
    for h in range(width // HEAD):
        col = pl.ds(h * HEAD, HEAD)
        for i, (low, high) in enumerate(pairs):
            rows = pl.ds(i * n, n)

            def fill(blk, rows=rows, col=col):
                k_all[rows, :] = normed(blk[pl.ds(0, n), col], ks_ref[rows, :], kg_ref[:, col])
                v_all[rows, :] = blk[pl.ds(n, n), col]

            if high is None:
                fill(low)
            else:
                pl.when(zl >= i)(lambda low=low: fill(low))
                pl.when(zl < i)(lambda high=high: fill(high))
        q = normed(q_ref[:, col], qs_ref[...], qg_ref[:, col])
        out_ref[:, col] = softmax_times(contract_last(q, k_all[...]), v_all[...])


def spatial(zl, q, qs, ks, qg, kg, blocks):
    n, width = q.shape
    heads = width // HEAD
    vmem = pl.BlockSpec(memory_space=pltpu.VMEM)
    return pl.pallas_call(
        spatial_kernel,
        out_shape=jax.ShapeDtypeStruct((n, width), jnp.float32),
        in_specs=[pl.BlockSpec(memory_space=pltpu.SMEM)] + [vmem] * (5 + len(blocks)),
        out_specs=vmem,
        scratch_shapes=[
            pltpu.VMEM((4 * n, HEAD), jnp.bfloat16),
            pltpu.VMEM((4 * n, HEAD), jnp.bfloat16),
        ],
        compiler_params=pltpu.CompilerParams(vmem_limit_bytes=40 << 20),
        cost_estimate=pl.CostEstimate(
            flops=heads * n * n * 4 * HEAD * 4, bytes_accessed=n * width * 22, transcendentals=heads * n * n * 4
        ),
    )(zl, q, qs, ks, qg, kg, *blocks)


def temporal_kernel(x_ref, out_ref, *, per):
    n, width = out_ref.shape
    row = lax.broadcasted_iota(jnp.int32, (n, n), 0)
    column = lax.broadcasted_iota(jnp.int32, (n, n), 1)
    same = (row - column) % per == 0
    for h in range(width // HEAD):
        q, k, v = (x_ref[:, pl.ds(i * width + h * HEAD, HEAD)] for i in range(3))
        scores = jnp.where(same, contract_last(q, k), -1e30)
        out_ref[:, pl.ds(h * HEAD, HEAD)] = softmax_times(scores, v).astype(jnp.bfloat16)


def temporal(x, per):
    n, width = x.shape
    width = width // 3
    heads = width // HEAD
    vmem = pl.BlockSpec(memory_space=pltpu.VMEM)
    return pl.pallas_call(
        lambda *refs: temporal_kernel(*refs, per=per),
        out_shape=jax.ShapeDtypeStruct((n, width), jnp.bfloat16),
        in_specs=[vmem],
        out_specs=vmem,
        compiler_params=pltpu.CompilerParams(vmem_limit_bytes=24 << 20),
        cost_estimate=pl.CostEstimate(
            flops=heads * n * n * HEAD * 4, bytes_accessed=n * width * 8, transcendentals=heads * n * n
        ),
    )(x)


def per_device(queries, keys, values, query_gain, key_gain):
    tok, width = queries.shape
    half = width // 2
    zl, core = lax.axis_index("zl"), lax.axis_index("c")
    frames = lax.axis_size(FRAME)

    def mine(a):
        return lax.dynamic_slice_in_dim(a, core * half, half, a.ndim - 1)

    def other(a):
        return lax.dynamic_slice_in_dim(a, (1 - core) * half, half, a.ndim - 1)

    swap = [(0, 1), (1, 0)]
    sent = jnp.concatenate([other(keys), other(values), other(queries)], axis=0)
    got = lax.ppermute(sent, "c", swap)
    part = jnp.stack(
        [
            jnp.sum(jnp.square(queries.astype(jnp.float32)), axis=1),
            jnp.sum(jnp.square(keys.astype(jnp.float32)), axis=1),
        ]
    )
    own_kv = jnp.concatenate([mine(keys), got[:tok], mine(values), got[tok : 2 * tok]], axis=0)
    own_q = jnp.concatenate([mine(queries), got[2 * tok :]], axis=0)
    part, own_kv = lax.optimization_barrier((part, own_kv))

    up = [(i, i + 1) for i in range(3)]
    down = [(i + 1, i) for i in range(3)]
    plus1 = lax.ppermute(own_kv, "zl", up)
    minus1 = lax.ppermute(own_kv, "zl", down)
    plus2 = lax.ppermute(plus1, "zl", up[1:])
    minus2 = lax.ppermute(minus1, "zl", down[:-1])
    plus3 = lax.ppermute(plus2, "zl", up[2:])
    minus3 = lax.ppermute(minus2, "zl", down[:1])

    stat = lax.psum(part, "tp")
    q_norm = normed(queries, stat[0][:, None], query_gain[None, :])
    k_norm = normed(keys, stat[1][:, None], key_gain[None, :])
    twin = lax.ppermute(stat, "c", swap)
    both = jnp.concatenate([stat[1], twin[1]])
    k_stats = [both] + [
        lax.ppermute(both, "zl", [(i, (i + j) % 4) for i in range(4)]) for j in range(1, 4)
    ]

    def to_positions(a):
        sent = a.reshape(frames, tok // frames, a.shape[1])
        return lax.all_to_all(sent, FRAME, 0, 0, tiled=True).reshape(a.shape)

    t_in = to_positions(jnp.concatenate([q_norm, k_norm, values], axis=1))
    t_back = to_positions(temporal(t_in, tok // frames))

    blocks = [own_kv, plus1, minus3, plus2, minus2, plus3, minus1]
    q_stat = jnp.concatenate([stat[0], twin[0]])[:, None]
    k_stat = jnp.concatenate(k_stats)[:, None]
    s_out = spatial(
        zl.reshape(1), own_q, q_stat, k_stat, mine(query_gain)[None], mine(key_gain)[None], blocks
    )
    s_got = lax.ppermute(s_out[tok:], "c", swap)
    s_mine = s_out[:tok]
    s_all = jnp.where(
        core == 0,
        jnp.concatenate([s_mine, s_got], axis=1),
        jnp.concatenate([s_got, s_mine], axis=1),
    )
    return (s_all + t_back.astype(jnp.float32)).astype(jnp.bfloat16)


def solution(mesh):
    axes = SEQ + ("tp",)
    split = Mesh(mesh.devices.reshape(4, 2, 2, 4, 2, 4), axes)
    return jax.shard_map(
        per_device,
        mesh=split,
        in_specs=(P(SEQ, "tp"), P(SEQ, "tp"), P(SEQ, "tp"), P("tp"), P("tp")),
        out_specs=P(SEQ, "tp"),
        check_vma=False,
    )
```

time: 178 us -> 115 us (0.65)
  blocking collectives: 74.9 us -> 8.2 us
  starting transfers between devices: 55.7 us -> 60.2 us
  waiting for transfers between devices: 24.2 us -> 28.7 us
  other arithmetic: 7.54 us -> 3.56 us
    psum x1, blocking collectives: 74.9 us -> 8.2 us  [per_device(): stat = lax.psum(part, 'tp')]
    ppermute x0 -> x4, starting transfers between devices: none -> 20.3 us  [the longest x3 15.5 us: per_device(): lax.ppermute(both, 'zl', [(i, (i + j) % 4) for i in range(4)])]
    all_to_all x4 -> x2, waiting for transfers between devices: 14.6 us -> 0.01 us  [to_positions(): return lax.all_to_all(sent, FRAME, 0, 0, tiled=True).reshape(a.shape)]
    ppermute x1, waiting for transfers between devices: 0.01 us -> 11.3 us  [per_device(): minus3 = lax.ppermute(minus2, 'zl', down[:1])]
    all_to_all x4 -> x2, starting transfers between devices: 27.3 us -> 19.1 us  [to_positions(): return lax.all_to_all(sent, FRAME, 0, 0, tiled=True).reshape(a.shape)]
    ppermute x1, starting transfers between devices: 11.3 us -> 3.54 us  [per_device(): s_got = lax.ppermute(s_out[tok:], 'c', swap)]
    ppermute x0 -> x4, waiting for transfers between devices: none -> 3.79 us  [the longest x3 3.79 us: per_device(): lax.ppermute(both, 'zl', [(i, (i + j) % 4) for i in range(4)])]
    select_n x4 -> x0, other arithmetic: 3.6 us -> none  [the longest x1 1.18 us: per_device(): jnp.where(zl >= 3, plus3, minus1)]
  transfers between devices with their start and end apart: 12 -> 14, of which waited for: 4 -> 5; matrix products, arithmetic and copies ran while one was open for 5% -> 2% of each run, Pallas kernels for 6% -> 9%
where the time goes in v2:
time: 115 us
  starting transfers between devices  60.2 us (52%)
  waiting for transfers between devices  28.7 us (25%)
  Pallas kernels  10.8 us (9%)
  blocking collectives  8.2 us (7%)
  other arithmetic  3.56 us (3%)
  local copies, waits for them, and re-layouts  2.95 us (3%)
    all_to_all x2, starting transfers between devices, to_positions(): return lax.all_to_all(sent, FRAME, 0, 0, tiled=True).reshape(a.shape)  19.1 us
    ppermute x3, starting transfers between devices, per_device(): lax.ppermute(both, 'zl', [(i, (i + j) % 4) for i in range(4)])  15.5 us
    ppermute x1, waiting for transfers between devices, per_device(): minus3 = lax.ppermute(minus2, 'zl', down[:1])  11.3 us
    ppermute x1, waiting for transfers between devices, per_device(): minus2 = lax.ppermute(minus1, 'zl', down[:-1])  11.2 us
    ppermute x1, starting transfers between devices, per_device(): got = lax.ppermute(sent, 'c', swap)  8.92 us
    psum x1, blocking collectives, per_device(): stat = lax.psum(part, 'tp')  8.2 us
    pallas_call x1, Pallas kernels, spatial(): pl.pallas_call(spatial_kernel, out_shape=jax.ShapeDtypeStruct((n, width),...  7.53 us
    ppermute x1, starting transfers between devices, per_device(): twin = lax.ppermute(stat, 'c', swap)  4.85 us
  transfers between devices with their start and end apart: 14, of which 5 were waited for; matrix products, arithmetic and copies ran while one was open for 2% of the time, Pallas kernels for 9%

profile of v2, /device:TPU:1, one launch (start us, length us, event | category | flops | bytes accessed | tf_op | source)
XLA Modules:
  0.0 114.8 jit_solution(4997431580078681505)
XLA Ops:
  0.0 1.0 constant_dynamic-slice_fusion.5
  1.0 1.3 %constant_dynamic-slice_fusion = (bf16[128,640]{1,0:T(8,128)(2,1)S(1)}, bf16[128,640]{1,0:T(8,128)(2,1)S(1)}, bf16[128,640]{1,0:T(8,128)(2,1)S(1)}, bf16[128,640]{1,0:T(8,128)(2,1)S(1)}) fusion(bf16[128,1280]{1,0:T(8,128)(2,1)} %param.7, s32[]{:T(128)S(6)} %select_n.21, s32[]{:T(128)S(6)} %select_n.22, bf16[128,1280]{1,0:T(8,128)(2,1)} %param.6), kind=kLoop, calls=%fused_computation.22 | loop fusion | bytes 1310728 | tf_op jit(solution)/shard_map/dynamic_slice | solution.py:112
  2.4 8.9 %collective-permute-start = (bf16[384,640]{1,0:T(8,128)(2,1)S(1)}, bf16[384,640]{1,0:T(8,128)(2,1)S(1)}, u32[]{:S(2)}, u32[]{:S(2)}) collective-permute-start(bf16[384,640]{1,0:T(8,128)(2,1)S(1)} %pad_maximum_fusion.1), channel_id=1, source_target_pairs={{0,4},{4,0},{1,5},{5,1},{2,6},{6,2},{3,7},{7,3},{8,12},{12,8},{9,1... | collective-permute-start | bytes 1474568 | tf_op jit(solution)/shard_map/ppermute | solution.py:119
  11.3 0.1 fusion
  11.5 0.1 fusion.3
  11.6 1.1 collective-permute-done
  12.9 1.5 %collective-permute-start.5 = (bf16[512,640]{1,0:T(8,128)(2,1)S(1)}, bf16[512,640]{1,0:T(8,128)(2,1)S(1)}, u32[]{:S(2)}, u32[]{:S(2)}) collective-permute-start(bf16[512,640]{1,0:T(8,128)(2,1)S(1)} %pad_maximum_fusion.own), channel_id=1, source_target_pairs={{0,8},{8,16},{16,24},{1,9},{9,17},{17,25},{2,10},{10,18},{18,26},{... | collective-permute-start | bytes 1966088 | tf_op jit(solution)/shard_map/ppermute | solution.py:132
  14.4 1.3 %collective-permute-start.6 = (bf16[512,640]{1,0:T(8,128)(2,1)S(1)}, bf16[512,640]{1,0:T(8,128)(2,1)}, u32[]{:S(2)}, u32[]{:S(2)}) collective-permute-start(bf16[512,640]{1,0:T(8,128)(2,1)S(1)} %pad_maximum_fusion.own), channel_id=1, source_target_pairs={{8,0},{16,8},{24,16},{9,1},{17,9},{25,17},{10,2},{18,10},{26,18},{... | collective-permute-start | bytes 1966088 | tf_op jit(solution)/shard_map/ppermute | solution.py:133
  15.7 8.2 %psum.7 = f32[2,128]{1,0:T(2,128)S(1)} all-reduce(f32[2,128]{1,0:T(2,128)S(1)} %pad_maximum_fusion.3), channel_id=1, replica_groups=mesh['x'=4,'yl'=2,'zh'=2,'zl'=4,'c'=2,'tp'=4] {'tp'}, use_global_device_ids=true, to_apply=%region_2.0 | all-reduce | flops 256 | bytes 2048 | tf_op jit(solution)/shard_map/psum | solution.py:139
  23.9 0.1 fusion.2
  24.1 0.1 fusion.5
  24.2 1.0 maximum_bitcast_fusion
  25.2 11.8 %all-to-all-start = ((bf16[16,8,3840]{2,1,0:T(8,128)(2,1)}), bf16[16,8,3840]{2,1,0:T(8,128)(2,1)S(1)}, u32[]{:S(2)}, u32[]{:S(2)}) async-start(bf16[16,8,3840]{2,1,0:T(8,128)(2,1)} %maximum_bitcast_fusion), calls=%async_computation | async-start | bytes 1966080 | tf_op jit(solution)/shard_map/all_to_all | solution.py:150
  37.2 4.8 %collective-permute-start.1 = (f32[2,128]{1,0:T(2,128)S(1)}, f32[2,128]{1,0:T(2,128)S(1)}, u32[]{:S(2)}, u32[]{:S(2)}) collective-permute-start(f32[2,128]{1,0:T(2,128)S(1)} %psum.7), channel_id=1, source_target_pairs={{0,4},{4,0},{1,5},{5,1},{2,6},{6,2},{3,7},{7,3},{8,12},{12,8},{9,1... | collective-permute-start | bytes 3080 | tf_op jit(solution)/shard_map/ppermute | solution.py:142
  42.1 1.5 %collective-permute-start.9 = (bf16[512,640]{1,0:T(8,128)(2,1)S(1)}, bf16[512,640]{1,0:T(8,128)(2,1)}, u32[]{:S(2)}, u32[]{:S(2)}) collective-permute-start(bf16[512,640]{1,0:T(8,128)(2,1)S(1)} %collective-permute-done.5.p1), channel_id=1, source_target_pairs={{8,16},{16,24},{9,17},{17,25},{10,18},{18,26},{11,19},{19,27},{12,... | collective-permute-start | bytes 1966088 | tf_op jit(solution)/shard_map/ppermute | solution.py:134
  43.6 1.3 %collective-permute-start.7 = (bf16[512,640]{1,0:T(8,128)(2,1)}, bf16[512,640]{1,0:T(8,128)(2,1)}, u32[]{:S(2)}, u32[]{:S(2)}) collective-permute-start(bf16[512,640]{1,0:T(8,128)(2,1)} %collective-permute-done.6.m1), channel_id=1, source_target_pairs={{8,0},{16,8},{9,1},{17,9},{10,2},{18,10},{11,3},{19,11},{12,4},{20... | collective-permute-start | bytes 1966088 | tf_op jit(solution)/shard_map/ppermute | solution.py:135
  45.0 7.3 %collective-permute-start.2 = (f32[256]{0:T(256)S(1)}, f32[256]{0:T(256)S(1)}, u32[]{:S(2)}, u32[]{:S(2)}) collective-permute-start(f32[256]{0:T(256)S(1)} %pad_maximum_fusion.5), channel_id=1, source_target_pairs={{0,8},{8,16},{16,24},{24,0},{1,9},{9,17},{17,25},{25,1},{2,10},{10... | collective-permute-start | bytes 3080 | tf_op jit(solution)/shard_map/ppermute | solution.py:145
  52.3 3.9 %collective-permute-start.3 = (f32[256]{0:T(256)S(1)}, f32[256]{0:T(256)S(1)}, u32[]{:S(2)}, u32[]{:S(2)}) collective-permute-start(f32[256]{0:T(256)S(1)} %pad_maximum_fusion.5), channel_id=1, source_target_pairs={{0,16},{8,24},{16,0},{24,8},{1,17},{9,25},{17,1},{25,9},{2,18},{10... | collective-permute-start | bytes 3080 | tf_op jit(solution)/shard_map/ppermute | solution.py:145
  56.2 4.3 %collective-permute-start.4 = (f32[256]{0:T(256)S(1)}, f32[256]{0:T(256)S(1)}, u32[]{:S(2)}, u32[]{:S(2)}) collective-permute-start(f32[256]{0:T(256)S(1)} %pad_maximum_fusion.5), channel_id=1, source_target_pairs={{0,24},{8,0},{16,8},{24,16},{1,25},{9,1},{17,9},{25,17},{2,26},{10... | collective-permute-start | bytes 3080 | tf_op jit(solution)/shard_map/ppermute | solution.py:145
  60.5 1.5 %collective-permute-start.10 = (bf16[512,640]{1,0:T(8,128)(2,1)}, bf16[512,640]{1,0:T(8,128)(2,1)}, u32[]{:S(2)}, u32[]{:S(2)}) collective-permute-start(bf16[512,640]{1,0:T(8,128)(2,1)} %collective-permute-done.9.p2), channel_id=1, source_target_pairs={{16,24},{17,25},{18,26},{19,27},{20,28},{21,29},{22,30},{23,31},{4... | collective-permute-start | bytes 1966088 | tf_op jit(solution)/shard_map/ppermute | solution.py:136
  62.0 11.2 %collective-permute-done.7.m2 = bf16[512,640]{1,0:T(8,128)(2,1)} collective-permute-done((bf16[512,640]{1,0:T(8,128)(2,1)}, bf16[512,640]{1,0:T(8,128)(2,1)}, u32[]{:S(2)}, u32[]{:S(2)}) %collective-permute-start.7) | collective-permute-done | bytes 655392 | tf_op jit(solution)/shard_map/ppermute | solution.py:135
  73.2 1.3 %collective-permute-start.8 = (bf16[512,640]{1,0:T(8,128)(2,1)}, bf16[512,640]{1,0:T(8,128)(2,1)}, u32[]{:S(2)}, u32[]{:S(2)}) collective-permute-start(bf16[512,640]{1,0:T(8,128)(2,1)} %collective-permute-done.7.m2), channel_id=1, source_target_pairs={{8,0},{9,1},{10,2},{11,3},{12,4},{13,5},{14,6},{15,7},{40,32},{41,... | collective-permute-start | bytes 1966088 | tf_op jit(solution)/shard_map/ppermute | solution.py:137
  74.5 0.1 copy.6.qs_ref
  74.7 3.8 %collective-permute-done.3 = f32[256]{0:T(256)S(1)} collective-permute-done((f32[256]{0:T(256)S(1)}, f32[256]{0:T(256)S(1)}, u32[]{:S(2)}, u32[]{:S(2)}) %collective-permute-start.3) | collective-permute-done | bytes 1056 | tf_op jit(solution)/shard_map/ppermute | solution.py:145
  78.5 0.2 copy.7.ks_ref
  78.7 3.2 %shard_map.56 = bf16[128,1280]{1,0:T(8,128)(2,1)} custom-call(bf16[128,3840]{1,0:T(8,128)(2,1)S(1)} %bitcast.28), custom_call_target="tpu_custom_call" | custom-call | flops 83886080 | bytes 1310720 | tf_op jit(solution)/shard_map/pallas_call | solution.py:93
  81.9 7.3 %all-to-all-start.1 = ((bf16[16,8,1280]{2,1,0:T(8,128)(2,1)}), bf16[16,8,1280]{2,1,0:T(8,128)(2,1)}, u32[]{:S(2)}, u32[]{:S(2)}) async-start(bf16[16,8,1280]{2,1,0:T(8,128)(2,1)} %bitcast.11), calls=%async_computation.1 | async-start | bytes 655360 | tf_op jit(solution)/shard_map/all_to_all | solution.py:150
  89.3 11.3 %collective-permute-done.8.m3 = bf16[512,640]{1,0:T(8,128)(2,1)} collective-permute-done((bf16[512,640]{1,0:T(8,128)(2,1)}, bf16[512,640]{1,0:T(8,128)(2,1)}, u32[]{:S(2)}, u32[]{:S(2)}) %collective-permute-start.8) | collective-permute-done | bytes 655392 | tf_op jit(solution)/shard_map/ppermute | solution.py:137
  100.6 7.5 %shard_map.55 = f32[256,640]{1,0:T(8,128)S(1)} custom-call(s32[1]{0:T(128)} %bitcast.zl_ref, bf16[256,640]{1,0:T(8,128)(2,1)S(1)} %pad_maximum_fusion.2.q_ref, f32[256,1]{1,0:T(8,128)S(1)} %copy.6.qs_ref, f32[1024,1]{1,0:T(8,128)S(1)} %copy.7.ks_ref, f32[1,640]{1,0:T(1,128)S(1)} %broadcast_in_dim.16.qg_ref, f32[1,640]{1,0:T(1,128)S(1)} %broadcast_in_dim.17.kg_ref, ...), custom_call_target="tpu_custom_call" | custom-call | flops 671088640 | bytes 3604480 | tf_op jit(solution)/shard_map/pallas_call | solution.py:61
  108.2 3.5 %collective-permute-start.11 = (f32[128,640]{1,0:T(8,128)S(1)}, f32[128,640]{1,0:T(8,128)S(1)}, u32[]{:S(2)}, u32[]{:S(2)}) collective-permute-start(f32[128,640]{1,0:T(8,128)S(1)} %get-tuple-element.10), channel_id=1, source_target_pairs={{0,4},{4,0},{1,5},{5,1},{2,6},{6,2},{3,7},{7,3},{8,12},{12,8},{9,1... | collective-permute-start | bytes 983048 | tf_op jit(solution)/shard_map/ppermute | solution.py:161
  111.8 1.2 %collective-permute-done.11 = f32[128,640]{1,0:T(8,128)S(1)} collective-permute-done((f32[128,640]{1,0:T(8,128)S(1)}, f32[128,640]{1,0:T(8,128)S(1)}, u32[]{:S(2)}, u32[]{:S(2)}) %collective-permute-start.11) | collective-permute-done | bytes 327712 | tf_op jit(solution)/shard_map/ppermute | solution.py:161
  113.0 1.8 %fusion.7 = bf16[128,1280]{1,0:T(8,128)(2,1)} fusion(f32[128,640]{1,0:T(8,128)S(1)} %collective-permute-done.11, f32[128,640]{1,0:T(8,128)S(1)} %get-tuple-element.9, bf16[16,8,1280]{2,1,0:T(8,128)(2,1)} %all-to-all-done.1, pred[]{:T(512)S(6)} %eq.3), kind=kLoop, calls=%fused_computation.14 | loop fusion | flops 983040 | bytes 1310721 | tf_op jit(solution)/shard_map/convert_element_type | solution.py:168
  (39 shorter events, 0.5 us)
Async XLA Ops:
  1.0 10.3 %copy-start = (bf16[128,1280]{1,0:T(8,128)(2,1)S(1)}, bf16[128,1280]{1,0:T(8,128)(2,1)}, u32[]{:S(2)}) copy-start(bf16[128,1280]{1,0:T(8,128)(2,1)} %param.5) | copy-start | bytes 983044
  2.3 9.2 %copy-start.1 = (bf16[128,1280]{1,0:T(8,128)(2,1)S(1)}, bf16[128,1280]{1,0:T(8,128)(2,1)}, u32[]{:S(2)}) copy-start(bf16[128,1280]{1,0:T(8,128)(2,1)} %param.6) | copy-start | bytes 983044
  2.4 10.4 %collective-permute-start = (bf16[384,640]{1,0:T(8,128)(2,1)S(1)}, bf16[384,640]{1,0:T(8,128)(2,1)S(1)}, u32[]{:S(2)}, u32[]{:S(2)}) collective-permute-start(bf16[384,640]{1,0:T(8,128)(2,1)S(1)} %pad_maximum_fusion.1), channel_id=1, source_target_pairs={{0,4},{4,0},{1,5},{5,1},{2,6},{6,2},{3,7},{7,3},{8,12},{12,8},{9,1... | collective-permute-start | bytes 1474568 | tf_op jit(solution)/shard_map/ppermute | solution.py:119
  11.6 12.3 %copy-start.3 = (f32[1280]{0:T(1024)S(1)}, f32[1280]{0:T(1024)}, u32[]{:S(2)}) copy-start(f32[1280]{0:T(1024)} %param.8) | copy-start | bytes 15364
  12.8 11.2 %copy-start.4 = (f32[1280]{0:T(1024)S(1)}, f32[1280]{0:T(1024)}, u32[]{:S(2)}) copy-start(f32[1280]{0:T(1024)} %param.9) | copy-start | bytes 15364
  12.9 11.3 %copy-start.2 = (bf16[128,1280]{1,0:T(8,128)(2,1)S(1)}, bf16[128,1280]{1,0:T(8,128)(2,1)}, u32[]{:S(2)}) copy-start(bf16[128,1280]{1,0:T(8,128)(2,1)} %param.7) | copy-start | bytes 983044
  12.9 29.1 %collective-permute-start.5 = (bf16[512,640]{1,0:T(8,128)(2,1)S(1)}, bf16[512,640]{1,0:T(8,128)(2,1)S(1)}, u32[]{:S(2)}, u32[]{:S(2)}) collective-permute-start(bf16[512,640]{1,0:T(8,128)(2,1)S(1)} %pad_maximum_fusion.own), channel_id=1, source_target_pairs={{0,8},{8,16},{16,24},{1,9},{9,17},{17,25},{2,10},{10,18},{18,26},{... | collective-permute-start | bytes 1966088 | tf_op jit(solution)/shard_map/ppermute | solution.py:132
  14.4 29.2 %collective-permute-start.6 = (bf16[512,640]{1,0:T(8,128)(2,1)S(1)}, bf16[512,640]{1,0:T(8,128)(2,1)}, u32[]{:S(2)}, u32[]{:S(2)}) collective-permute-start(bf16[512,640]{1,0:T(8,128)(2,1)S(1)} %pad_maximum_fusion.own), channel_id=1, source_target_pairs={{8,0},{16,8},{24,16},{9,1},{17,9},{25,17},{10,2},{18,10},{26,18},{... | collective-permute-start | bytes 1966088 | tf_op jit(solution)/shard_map/ppermute | solution.py:133
  25.2 53.5 %all-to-all-start = ((bf16[16,8,3840]{2,1,0:T(8,128)(2,1)}), bf16[16,8,3840]{2,1,0:T(8,128)(2,1)S(1)}, u32[]{:S(2)}, u32[]{:S(2)}) async-start(bf16[16,8,3840]{2,1,0:T(8,128)(2,1)} %maximum_bitcast_fusion), calls=%async_computation | async-start | bytes 1966080 | tf_op jit(solution)/shard_map/all_to_all | solution.py:150
  37.2 7.7 %collective-permute-start.1 = (f32[2,128]{1,0:T(2,128)S(1)}, f32[2,128]{1,0:T(2,128)S(1)}, u32[]{:S(2)}, u32[]{:S(2)}) collective-permute-start(f32[2,128]{1,0:T(2,128)S(1)} %psum.7), channel_id=1, source_target_pairs={{0,4},{4,0},{1,5},{5,1},{2,6},{6,2},{3,7},{7,3},{8,12},{12,8},{9,1... | collective-permute-start | bytes 3080 | tf_op jit(solution)/shard_map/ppermute | solution.py:142
  42.1 18.4 %collective-permute-start.9 = (bf16[512,640]{1,0:T(8,128)(2,1)S(1)}, bf16[512,640]{1,0:T(8,128)(2,1)}, u32[]{:S(2)}, u32[]{:S(2)}) collective-permute-start(bf16[512,640]{1,0:T(8,128)(2,1)S(1)} %collective-permute-done.5.p1), channel_id=1, source_target_pairs={{8,16},{16,24},{9,17},{17,25},{10,18},{18,26},{11,19},{19,27},{12,... | collective-permute-start | bytes 1966088 | tf_op jit(solution)/shard_map/ppermute | solution.py:134
  43.6 29.6 %collective-permute-start.7 = (bf16[512,640]{1,0:T(8,128)(2,1)}, bf16[512,640]{1,0:T(8,128)(2,1)}, u32[]{:S(2)}, u32[]{:S(2)}) collective-permute-start(bf16[512,640]{1,0:T(8,128)(2,1)} %collective-permute-done.6.m1), channel_id=1, source_target_pairs={{8,0},{16,8},{9,1},{17,9},{10,2},{18,10},{11,3},{19,11},{12,4},{20... | collective-permute-start | bytes 1966088 | tf_op jit(solution)/shard_map/ppermute | solution.py:135
  45.0 29.7 %collective-permute-start.2 = (f32[256]{0:T(256)S(1)}, f32[256]{0:T(256)S(1)}, u32[]{:S(2)}, u32[]{:S(2)}) collective-permute-start(f32[256]{0:T(256)S(1)} %pad_maximum_fusion.5), channel_id=1, source_target_pairs={{0,8},{8,16},{16,24},{24,0},{1,9},{9,17},{17,25},{25,1},{2,10},{10... | collective-permute-start | bytes 3080 | tf_op jit(solution)/shard_map/ppermute | solution.py:145
  52.3 26.2 %collective-permute-start.3 = (f32[256]{0:T(256)S(1)}, f32[256]{0:T(256)S(1)}, u32[]{:S(2)}, u32[]{:S(2)}) collective-permute-start(f32[256]{0:T(256)S(1)} %pad_maximum_fusion.5), channel_id=1, source_target_pairs={{0,16},{8,24},{16,0},{24,8},{1,17},{9,25},{17,1},{25,9},{2,18},{10... | collective-permute-start | bytes 3080 | tf_op jit(solution)/shard_map/ppermute | solution.py:145
  56.2 22.3 %collective-permute-start.4 = (f32[256]{0:T(256)S(1)}, f32[256]{0:T(256)S(1)}, u32[]{:S(2)}, u32[]{:S(2)}) collective-permute-start(f32[256]{0:T(256)S(1)} %pad_maximum_fusion.5), channel_id=1, source_target_pairs={{0,24},{8,0},{16,8},{24,16},{1,25},{9,1},{17,9},{25,17},{2,26},{10... | collective-permute-start | bytes 3080 | tf_op jit(solution)/shard_map/ppermute | solution.py:145
  60.5 28.8 %collective-permute-start.10 = (bf16[512,640]{1,0:T(8,128)(2,1)}, bf16[512,640]{1,0:T(8,128)(2,1)}, u32[]{:S(2)}, u32[]{:S(2)}) collective-permute-start(bf16[512,640]{1,0:T(8,128)(2,1)} %collective-permute-done.9.p2), channel_id=1, source_target_pairs={{16,24},{17,25},{18,26},{19,27},{20,28},{21,29},{22,30},{23,31},{4... | collective-permute-start | bytes 1966088 | tf_op jit(solution)/shard_map/ppermute | solution.py:136
  73.2 27.5 %collective-permute-start.8 = (bf16[512,640]{1,0:T(8,128)(2,1)}, bf16[512,640]{1,0:T(8,128)(2,1)}, u32[]{:S(2)}, u32[]{:S(2)}) collective-permute-start(bf16[512,640]{1,0:T(8,128)(2,1)} %collective-permute-done.7.m2), channel_id=1, source_target_pairs={{8,0},{9,1},{10,2},{11,3},{12,4},{13,5},{14,6},{15,7},{40,32},{41,... | collective-permute-start | bytes 1966088 | tf_op jit(solution)/shard_map/ppermute | solution.py:137
  81.9 31.1 %all-to-all-start.1 = ((bf16[16,8,1280]{2,1,0:T(8,128)(2,1)}), bf16[16,8,1280]{2,1,0:T(8,128)(2,1)}, u32[]{:S(2)}, u32[]{:S(2)}) async-start(bf16[16,8,1280]{2,1,0:T(8,128)(2,1)} %bitcast.11), calls=%async_computation.1 | async-start | bytes 655360 | tf_op jit(solution)/shard_map/all_to_all | solution.py:150
  108.2 4.8 %collective-permute-start.11 = (f32[128,640]{1,0:T(8,128)S(1)}, f32[128,640]{1,0:T(8,128)S(1)}, u32[]{:S(2)}, u32[]{:S(2)}) collective-permute-start(f32[128,640]{1,0:T(8,128)S(1)} %get-tuple-element.10), channel_id=1, source_target_pairs={{0,4},{4,0},{1,5},{5,1},{2,6},{6,2},{3,7},{7,3},{8,12},{12,8},{9,1... | collective-permute-start | bytes 983048 | tf_op jit(solution)/shard_map/ppermute | solution.py:161

commit v3 on v2

v3 whole, which is shorter than its diff:
```python
import math

import jax
import jax.numpy as jnp
from jax import lax
from jax.experimental import pallas as pl
from jax.experimental.pallas import tpu as pltpu
from jax.sharding import Mesh, PartitionSpec as P

D = 5120
HEAD = 128
EPS = 1e-06
SCALE = 1.0 / math.sqrt(HEAD)
SEQ = ("x", "yl", "zh", "zl", "c")
FRAME = ("x", "yl", "zh")


def contract_last(a, b):
    return lax.dot_general(a, b, (((1,), (1,)), ((), ())), preferred_element_type=jnp.float32)


def softmax_times(scores, v):
    top = jnp.max(scores, axis=-1, keepdims=True)
    raised = jnp.exp((scores - top) * SCALE)
    total = jnp.sum(raised, axis=-1, keepdims=True)
    out = jnp.dot(raised.astype(jnp.bfloat16), v, preferred_element_type=jnp.float32)
    return out / total


def normed(x, stat, gain):
    scale = lax.rsqrt(stat / D + EPS)
    return (x.astype(jnp.float32) * scale * gain).astype(jnp.bfloat16)


def prep_kernel(at_ref, q_ref, k_ref, v_ref, p0, p1, p2, p3, sum_ref):
    n, width = q_ref.shape
    half = width // 2
    for j, out in enumerate((p0, p1, p2, p3)):
        h = lax.rem(at_ref[0] + j, 4) * HEAD
        for c, side in enumerate((at_ref[1], 1 - at_ref[1])):
            moving = pl.ds(pl.multiple_of(side * half + h, HEAD), HEAD)
            staying = pl.ds(pl.multiple_of((side + 1) * half - HEAD, HEAD), HEAD)
            parts = ((q_ref, moving), (k_ref, moving), (v_ref, moving), (k_ref, staying), (v_ref, staying))
            for i, (ref, col) in enumerate(parts):
                out[:, c * half + i * HEAD : c * half + (i + 1) * HEAD] = ref[:, col]
    ones = jnp.ones((4, HEAD), jnp.float32)
    for i, ref in enumerate((q_ref, k_ref)):
        total = jnp.zeros((n, HEAD), jnp.float32)
        for h in range(width // HEAD):
            total += jnp.square(ref[:, h * HEAD : (h + 1) * HEAD].astype(jnp.float32))
        sum_ref[i * 4 : (i + 1) * 4, :] = lax.dot_general(
            ones,
            total,
            (((1,), (1,)), ((), ())),
            precision=lax.Precision.HIGHEST,
            preferred_element_type=jnp.float32,
        )


def prep(at, q, k, v):
    vmem = pl.BlockSpec(memory_space=pltpu.VMEM)
    return pl.pallas_call(
        prep_kernel,
        out_shape=[jax.ShapeDtypeStruct(q.shape, q.dtype)] * 4
        + [jax.ShapeDtypeStruct((8, q.shape[0]), jnp.float32)],
        in_specs=[pl.BlockSpec(memory_space=pltpu.SMEM)] + [vmem] * 3,
        out_specs=[vmem] * 5,
        compiler_params=pltpu.CompilerParams(vmem_limit_bytes=24 << 20),
        cost_estimate=pl.CostEstimate(flops=q.size * 4, bytes_accessed=q.size * 14, transcendentals=0),
    )(at, q, k, v)


def spatial_kernel(at_ref, b0, b1, b2, b3, q_last, s0, s2, s3, stat_ref, qg_ref, kg_ref, o0, o1, o2, o3, o_last, q_all, k_all, v_all):
    n, half = b0.shape[0], b0.shape[1] // 2
    zl, core = at_ref[0], at_ref[1]
    moving = pl.ds(pl.multiple_of(core * half + zl * HEAD, HEAD), HEAD)
    staying = pl.ds(pl.multiple_of(core * half + half - HEAD, HEAD), HEAD)
    q_gain, q_gain_last = qg_ref[:, moving], qg_ref[:, staying]
    k_gain, k_gain_last = kg_ref[:, moving], kg_ref[:, staying]
    for j, blk in enumerate((b0, b1, b2, b3)):
        for twin in range(2):

            def part(i):
                if twin:
                    ref, at = ((s0, 0), (s0, half), (s2, 0), (s3, 0))[j]
                    return ref[:, at + i * HEAD : at + (i + 1) * HEAD]
                return blk[:, i * HEAD : (i + 1) * HEAD]

            rows = slice((j * 2 + twin) * n, (j * 2 + twin + 1) * n)
            place = lax.rem(zl + 4 - j, 4) * 2 + (1 - core if twin else core)
            from_rows = pl.ds(pl.multiple_of(place * n, n), n)
            q_stat, k_stat = stat_ref[from_rows, 0:1], stat_ref[from_rows, 1:2]
            q_all[rows, 0:HEAD] = normed(part(0), q_stat, q_gain)
            k_all[rows, 0:HEAD] = normed(part(1), k_stat, k_gain)
            v_all[rows, 0:HEAD] = part(2)
            k_all[rows, HEAD:] = normed(part(3), k_stat, k_gain_last)
            v_all[rows, HEAD:] = part(4)
            if j == 0:
                q = s0[:, 2 * half :] if twin else q_last[...]
                q_all[rows, HEAD:] = normed(q, q_stat, q_gain_last)
    k_one, k_two = k_all[:, 0:HEAD], k_all[:, HEAD:]
    v_one, v_two = v_all[:, 0:HEAD], v_all[:, HEAD:]
    for j, out in enumerate((o0, o1, o2, o3)):
        q = q_all[j * 2 * n : (j + 1) * 2 * n, 0:HEAD]
        out[...] = softmax_times(contract_last(q, k_one), v_one).astype(jnp.bfloat16)
    o_last[...] = softmax_times(contract_last(q_all[0 : 2 * n, HEAD:], k_two), v_two).astype(jnp.bfloat16)


def spatial(at, blocks, q_last, swapped, stats, q_gain, k_gain):
    n = blocks[0].shape[0]
    vmem = pl.BlockSpec(memory_space=pltpu.VMEM)
    return pl.pallas_call(
        spatial_kernel,
        out_shape=[jax.ShapeDtypeStruct((2 * n, HEAD), jnp.bfloat16)] * 5,
        in_specs=[pl.BlockSpec(memory_space=pltpu.SMEM)] + [vmem] * 11,
        out_specs=[vmem] * 5,
        scratch_shapes=[pltpu.VMEM((8 * n, 2 * HEAD), jnp.bfloat16)] * 3,
        compiler_params=pltpu.CompilerParams(vmem_limit_bytes=40 << 20),
        cost_estimate=pl.CostEstimate(
            flops=5 * n * n * 64 * HEAD, bytes_accessed=n * HEAD * 120, transcendentals=5 * n * n * 16
        ),
    )(at, *blocks, q_last, *swapped, stats, q_gain, k_gain)


def temporal_kernel(x_ref, out_ref, *, per):
    n, width = out_ref.shape
    row = lax.broadcasted_iota(jnp.int32, (n, n), 0)
    column = lax.broadcasted_iota(jnp.int32, (n, n), 1)
    same = (row - column) % per == 0
    for h in range(width // HEAD):
        q, k, v = (x_ref[:, pl.ds(i * width + h * HEAD, HEAD)] for i in range(3))
        scores = jnp.where(same, contract_last(q, k), -1e30)
        out_ref[:, pl.ds(h * HEAD, HEAD)] = softmax_times(scores, v).astype(jnp.bfloat16)


def temporal(x, per):
    n, width = x.shape
    width = width // 3
    heads = width // HEAD
    vmem = pl.BlockSpec(memory_space=pltpu.VMEM)
    return pl.pallas_call(
        lambda *refs: temporal_kernel(*refs, per=per),
        out_shape=jax.ShapeDtypeStruct((n, width), jnp.bfloat16),
        in_specs=[vmem],
        out_specs=vmem,
        compiler_params=pltpu.CompilerParams(vmem_limit_bytes=24 << 20),
        cost_estimate=pl.CostEstimate(
            flops=heads * n * n * HEAD * 4, bytes_accessed=n * width * 8, transcendentals=heads * n * n
        ),
    )(x)


def per_device(queries, keys, values, query_gain, key_gain):
    tok, width = queries.shape
    half = width // 2
    zl, core = lax.axis_index("zl"), lax.axis_index("c")
    frames = lax.axis_size(FRAME)
    swap = [(0, 1), (1, 0)]

    def shift(a, j):
        return lax.ppermute(a, "zl", [(i, (i + j) % 4) for i in range(4)])

    def column(a, start, size=HEAD):
        return lax.dynamic_slice_in_dim(a, start, size, 1)

    def to_positions(a):
        sent = a.reshape(frames, tok // frames, a.shape[1])
        return lax.all_to_all(sent, FRAME, 0, 0, tiled=True).reshape(a.shape)

    at = jnp.stack([zl, core])
    *parts, sums = prep(at, queries, keys, values)
    blocks = [parts[0]] + [shift(parts[j], j) for j in (1, 2, 3)]
    sums = lax.psum(sums, "tp")

    q_norm = normed(queries, sums[0][:, None], query_gain[None, :])
    k_norm = normed(keys, sums[4][:, None], key_gain[None, :])
    t_sent = jnp.concatenate([q_norm, k_norm, values], axis=1)
    stat = jnp.stack([sums[0], sums[4]])
    stats = lax.all_gather(stat, ("zl", "c")).transpose(0, 2, 1).reshape(8 * tok, 2)
    t_sent, blocks, stats = lax.optimization_barrier((t_sent, blocks, stats))
    t_in = to_positions(t_sent)

    away = [b[:, half:] for b in blocks]
    q_away = column(queries, (2 - core) * half - HEAD)
    swapped = [
        lax.ppermute(a, "c", swap)
        for a in (jnp.concatenate([away[0], away[1], q_away], axis=1), away[2], away[3])
    ]
    outs = spatial(
        at,
        blocks,
        column(queries, (core + 1) * half - HEAD),
        swapped,
        stats,
        query_gain[None],
        key_gain[None],
    )
    t_in, last = lax.optimization_barrier((t_in, outs[4]))
    t_out = temporal(t_in, tok // frames)
    t_back = to_positions(t_out)

    moved = [shift(outs[j], 4 - j) for j in (1, 2, 3)]
    moved, t_out = lax.optimization_barrier((moved, t_out))
    heads = [outs[0]] + moved
    turned = column(jnp.concatenate(heads + heads[:3], axis=1), (4 - zl) % 4 * HEAD, 4 * HEAD)
    s_half = jnp.concatenate([turned, last], axis=1)
    s_got = lax.ppermute(s_half[tok:], "c", swap)
    s_mine = s_half[:tok]
    s_all = jnp.where(
        core == 0,
        jnp.concatenate([s_mine, s_got], axis=1),
        jnp.concatenate([s_got, s_mine], axis=1),
    )
    return (s_all.astype(jnp.float32) + t_back.astype(jnp.float32)).astype(jnp.bfloat16)


def solution(mesh):
    axes = SEQ + ("tp",)
    split = Mesh(mesh.devices.reshape(4, 2, 2, 4, 2, 4), axes)
    return jax.shard_map(
        per_device,
        mesh=split,
        in_specs=(P(SEQ, "tp"), P(SEQ, "tp"), P(SEQ, "tp"), P("tp"), P("tp")),
        out_specs=P(SEQ, "tp"),
        check_vma=False,
    )
```

time: 115 us -> 111 us (0.965)
  the two profiles are of different devices: /device:TPU:1 before, /device:TPU:80 now
where the time goes in v3:
time: 111 us; the launch traced here: 110 us
  starting transfers between devices  50.9 us (46%)
  blocking collectives  25 us (23%)
  waiting for transfers between devices  16.6 us (15%)
  Pallas kernels  9.52 us (9%)
  local copies, waits for them, and re-layouts  4.74 us (4%)
  other arithmetic  3.01 us (3%)
    ppermute x6, starting transfers between devices, shift(): return lax.ppermute(a, 'zl', [(i, (i + j) % 4) for i in range(4)])  23.3 us
    all_to_all x2, starting transfers between devices, to_positions(): return lax.all_to_all(sent, FRAME, 0, 0, tiled=True).reshape(a.shape)  19.6 us
    all_gather x1, blocking collectives, per_device(): lax.all_gather(stat, ('zl', 'c')).transpose(0, 2, 1).reshape(8 * tok, 2)  13.7 us
    all_to_all x2, waiting for transfers between devices, to_positions(): return lax.all_to_all(sent, FRAME, 0, 0, tiled=True).reshape(a.shape)  13.6 us
    psum x1, blocking collectives, per_device(): sums = lax.psum(sums, 'tp')  11.2 us
    ppermute x3, starting transfers between devices, per_device(): lax.ppermute(a, 'c', swap)  6.21 us
    pallas_call x1, Pallas kernels, spatial(): pl.pallas_call(spatial_kernel, out_shape=[jax.ShapeDtypeStruct((2 * n, HE...  4.48 us
    pallas_call x1, Pallas kernels, temporal(): pl.pallas_call(lambda *refs: temporal_kernel(*refs, per=per), out_shape=j...  3.23 us
  transfers between devices with their start and end apart: 12, of which 4 were waited for; matrix products, arithmetic and copies ran while one was open for 3% of the time, Pallas kernels for 7%

profile of v3, /device:TPU:80, one launch (start us, length us, event | category | flops | bytes accessed | tf_op | source)
XLA Modules:
  0.0 110.1 jit_solution(11747627897060827823)
XLA Ops:
  0.0 0.1 pad_add_fusion.at_ref
  0.1 1.0 copy-done
  1.1 1.0 copy-done.2
  2.0 1.0 copy-done.4
  3.0 1.8 %shard_map.55 = (bf16[128,1280]{1,0:T(8,128)(2,1)S(1)}, bf16[128,1280]{1,0:T(8,128)(2,1)}, bf16[128,1280]{1,0:T(8,128)(2,1)}, bf16[128,1280]{1,0:T(8,128)(2,1)S(1)}, f32[8,128]{1,0:T(8,128)S(1)}) custom-call(s32[2]{0:T(128)S(1)} %pad_add_fusion.at_ref, bf16[128,1280]{1,0:T(8,128)(2,1)S(1)} %copy-done, bf16[128,1280]{1,0:T(8,128)(2,1)S(1)} %copy-done.2, ...), custom_call_target="tpu_custom_call" | custom-call | flops 655360 | bytes 2293760 | tf_op jit(solution)/shard_map/pallas_call | solution.py:62
  4.8 4.4 %collective-permute-start = (bf16[128,1280]{1,0:T(8,128)(2,1)}, bf16[128,1280]{1,0:T(8,128)(2,1)S(1)}, u32[]{:S(2)}, u32[]{:S(2)}) collective-permute-start(bf16[128,1280]{1,0:T(8,128)(2,1)} %get-tuple-element.28), channel_id=1, source_target_pairs={{0,8},{8,16},{16,24},{24,0},{1,9},{9,17},{17,25},{25,1},{2,10},{10... | collective-permute-start | bytes 983048 | tf_op jit(solution)/shard_map/ppermute | solution.py:161
  9.2 3.7 %collective-permute-start.1 = (bf16[128,1280]{1,0:T(8,128)(2,1)}, bf16[128,1280]{1,0:T(8,128)(2,1)S(1)}, u32[]{:S(2)}, u32[]{:S(2)}) collective-permute-start(bf16[128,1280]{1,0:T(8,128)(2,1)} %get-tuple-element.29), channel_id=1, source_target_pairs={{0,16},{8,24},{16,0},{24,8},{1,17},{9,25},{17,1},{25,9},{2,18},{10... | collective-permute-start | bytes 983048 | tf_op jit(solution)/shard_map/ppermute | solution.py:161
  13.0 3.9 %collective-permute-start.2 = (bf16[128,1280]{1,0:T(8,128)(2,1)S(1)}, bf16[128,1280]{1,0:T(8,128)(2,1)S(1)}, u32[]{:S(2)}, u32[]{:S(2)}) collective-permute-start(bf16[128,1280]{1,0:T(8,128)(2,1)S(1)} %get-tuple-element.30), channel_id=1, source_target_pairs={{0,24},{8,0},{16,8},{24,16},{1,25},{9,1},{17,9},{25,17},{2,26},{10... | collective-permute-start | bytes 983048 | tf_op jit(solution)/shard_map/ppermute | solution.py:161
  16.9 11.2 %psum.7 = f32[8,128]{1,0:T(8,128)S(1)} all-reduce(f32[8,128]{1,0:T(8,128)S(1)} %get-tuple-element.26), channel_id=1, replica_groups=mesh['x'=4,'yl'=2,'zh'=2,'zl'=4,'c'=2,'tp'=4] {'tp'}, use_global_device_ids=true, to_apply=%region_0.0 | all-reduce | flops 1024 | bytes 8192 | tf_op jit(solution)/shard_map/psum | solution.py:173
  28.1 13.7 %all-gather.1 = f32[8,2,128]{2,1,0:T(2,128)S(1)} all-gather(f32[1,2,128]{2,1,0:T(2,128)S(1)} %maximum_bitcast_fusion), channel_id=2, replica_groups=mesh['x'=4,'yl'=2,'zh'=2,'zl'=4,'c'=2,'tp'=4] {'zl','c'}, dimensions={0}, use_global_device_ids=true | all-gather | bytes 9216 | tf_op jit(solution)/shard_map/all_gather | solution.py:179
  41.9 0.2 copy.7
  42.1 0.2 multiply_convert_fusion
  42.4 1.0 pad_maximum_fusion
  43.4 11.4 %all-to-all-start = ((bf16[16,8,3840]{2,1,0:T(8,128)(2,1)}), bf16[16,8,3840]{2,1,0:T(8,128)(2,1)S(1)}, u32[]{:S(2)}, u32[]{:S(2)}) async-start(bf16[16,8,3840]{2,1,0:T(8,128)(2,1)} %bitcast.18), calls=%async_computation | async-start | bytes 1966080 | tf_op jit(solution)/shard_map/all_to_all | solution.py:168
  55.0 0.8 pad_maximum_fusion.1
  55.7 1.9 %collective-permute-start.3 = (bf16[128,1408]{1,0:T(8,128)(2,1)}, bf16[128,1408]{1,0:T(8,128)(2,1)S(1)}, u32[]{:S(2)}, u32[]{:S(2)}) collective-permute-start(bf16[128,1408]{1,0:T(8,128)(2,1)} %pad_maximum_fusion.1), channel_id=1, source_target_pairs={{0,4},{4,0},{1,5},{5,1},{2,6},{6,2},{3,7},{7,3},{8,12},{12,8},{9,1... | collective-permute-start | bytes 1081352 | tf_op jit(solution)/shard_map/ppermute | solution.py:186
  57.6 0.7 slice.30
  58.3 2.4 %collective-permute-start.4 = (bf16[128,640]{1,0:T(8,128)(2,1)}, bf16[128,640]{1,0:T(8,128)(2,1)S(1)}, u32[]{:S(2)}, u32[]{:S(2)}) collective-permute-start(bf16[128,640]{1,0:T(8,128)(2,1)} %slice.30), channel_id=1, source_target_pairs={{0,4},{4,0},{1,5},{5,1},{2,6},{6,2},{3,7},{7,3},{8,12},{12,8},{9,1... | collective-permute-start | bytes 491528 | tf_op jit(solution)/shard_map/ppermute | solution.py:186
  60.7 0.7 slice.31
  61.4 1.9 %collective-permute-start.5 = (bf16[128,640]{1,0:T(8,128)(2,1)}, bf16[128,640]{1,0:T(8,128)(2,1)}, u32[]{:S(2)}, u32[]{:S(2)}) collective-permute-start(bf16[128,640]{1,0:T(8,128)(2,1)} %slice.31), channel_id=1, source_target_pairs={{0,4},{4,0},{1,5},{5,1},{2,6},{6,2},{3,7},{7,3},{8,12},{12,8},{9,1... | collective-permute-start | bytes 491528 | tf_op jit(solution)/shard_map/ppermute | solution.py:186
  63.4 1.6 %collective-permute-done.5.s3 = bf16[128,640]{1,0:T(8,128)(2,1)} collective-permute-done((bf16[128,640]{1,0:T(8,128)(2,1)}, bf16[128,640]{1,0:T(8,128)(2,1)}, u32[]{:S(2)}, u32[]{:S(2)}) %collective-permute-start.5) | collective-permute-done | bytes 163872 | tf_op jit(solution)/shard_map/ppermute | solution.py:186
  65.0 4.5 %shard_map.56 = (bf16[256,128]{1,0:T(8,128)(2,1)S(1)}, bf16[256,128]{1,0:T(8,128)(2,1)}, bf16[256,128]{1,0:T(8,128)(2,1)}, bf16[256,128]{1,0:T(8,128)(2,1)}, bf16[256,128]{1,0:T(8,128)(2,1)S(1)}) custom-call(s32[2]{0:T(128)S(1)} %pad_add_fusion.at_ref, bf16[128,1280]{1,0:T(8,128)(2,1)S(1)} %get-tuple-element.31.b0, ...), custom_call_target="tpu_custom_call" | custom-call | flops 671088640 | bytes 1966080 | tf_op jit(solution)/shard_map/pallas_call | solution.py:112
  69.5 1.9 %collective-permute-start.6 = (bf16[256,128]{1,0:T(8,128)(2,1)}, bf16[256,128]{1,0:T(8,128)(2,1)S(1)}, u32[]{:S(2)}, u32[]{:S(2)}) collective-permute-start(bf16[256,128]{1,0:T(8,128)(2,1)} %get-tuple-element.37), channel_id=1, source_target_pairs={{0,24},{8,0},{16,8},{24,16},{1,25},{9,1},{17,9},{25,17},{2,26},{10... | collective-permute-start | bytes 196616 | tf_op jit(solution)/shard_map/ppermute | solution.py:161
  71.4 6.0 %collective-permute-start.7 = (bf16[256,128]{1,0:T(8,128)(2,1)}, bf16[256,128]{1,0:T(8,128)(2,1)S(1)}, u32[]{:S(2)}, u32[]{:S(2)}) collective-permute-start(bf16[256,128]{1,0:T(8,128)(2,1)} %get-tuple-element.38), channel_id=1, source_target_pairs={{0,16},{8,24},{16,0},{24,8},{1,17},{9,25},{17,1},{25,9},{2,18},{10... | collective-permute-start | bytes 196616 | tf_op jit(solution)/shard_map/ppermute | solution.py:161
  77.4 3.3 %collective-permute-start.8 = (bf16[256,128]{1,0:T(8,128)(2,1)}, bf16[256,128]{1,0:T(8,128)(2,1)S(1)}, u32[]{:S(2)}, u32[]{:S(2)}) collective-permute-start(bf16[256,128]{1,0:T(8,128)(2,1)} %get-tuple-element.39), channel_id=1, source_target_pairs={{0,8},{8,16},{16,24},{24,0},{1,9},{9,17},{17,25},{25,1},{2,10},{10... | collective-permute-start | bytes 196616 | tf_op jit(solution)/shard_map/ppermute | solution.py:161
  80.8 2.4 %all-to-all-done = bf16[16,8,3840]{2,1,0:T(8,128)(2,1)S(1)} async-done(((bf16[16,8,3840]{2,1,0:T(8,128)(2,1)}), bf16[16,8,3840]{2,1,0:T(8,128)(2,1)S(1)}, u32[]{:S(2)}, u32[]{:S(2)}) %all-to-all-start) | async-done | bytes 983072 | tf_op jit(solution)/shard_map/all_to_all | solution.py:168
  83.2 3.2 %shard_map.57 = bf16[128,1280]{1,0:T(8,128)(2,1)} custom-call(bf16[128,3840]{1,0:T(8,128)(2,1)S(1)} %bitcast.16), custom_call_target="tpu_custom_call" | custom-call | flops 83886080 | bytes 1310720 | tf_op jit(solution)/shard_map/pallas_call | solution.py:141
  86.5 8.1 %all-to-all-start.1 = ((bf16[16,8,1280]{2,1,0:T(8,128)(2,1)}), bf16[16,8,1280]{2,1,0:T(8,128)(2,1)S(1)}, u32[]{:S(2)}, u32[]{:S(2)}) async-start(bf16[16,8,1280]{2,1,0:T(8,128)(2,1)} %bitcast.9), calls=%async_computation.1 | async-start | bytes 655360 | tf_op jit(solution)/shard_map/all_to_all | solution.py:168
  94.8 1.9 %collective-permute-start.9 = (bf16[128,640]{1,0:T(8,128)(2,1)S(1)}, bf16[128,640]{1,0:T(8,128)(2,1)S(1)}, u32[]{:S(2)}, u32[]{:S(2)}) collective-permute-start(bf16[128,640]{1,0:T(8,128)(2,1)S(1)} %get-tuple-element.48), channel_id=1, source_target_pairs={{0,4},{4,0},{1,5},{5,1},{2,6},{6,2},{3,7},{7,3},{8,12},{12,8},{9,1... | collective-permute-start | bytes 491528 | tf_op jit(solution)/shard_map/ppermute | solution.py:207
  96.7 1.4 %collective-permute-done.9 = bf16[128,640]{1,0:T(8,128)(2,1)S(1)} collective-permute-done((bf16[128,640]{1,0:T(8,128)(2,1)S(1)}, bf16[128,640]{1,0:T(8,128)(2,1)S(1)}, u32[]{:S(2)}, u32[]{:S(2)}) %collective-permute-start.9) | collective-permute-done | bytes 163872 | tf_op jit(solution)/shard_map/ppermute | solution.py:207
  98.1 11.2 %all-to-all-done.1 = bf16[16,8,1280]{2,1,0:T(8,128)(2,1)S(1)} async-done(((bf16[16,8,1280]{2,1,0:T(8,128)(2,1)}), bf16[16,8,1280]{2,1,0:T(8,128)(2,1)S(1)}, u32[]{:S(2)}, u32[]{:S(2)}) %all-to-all-start.1) | async-done | bytes 327712 | tf_op jit(solution)/shard_map/all_to_all | solution.py:168
  109.3 0.8 fusion
  (39 shorter events, 0.3 us)
Async XLA Ops:
  0.0 42.1 %copy-start.6 = (f32[1280]{0:T(1024)S(1)}, f32[1280]{0:T(1024)}, u32[]{:S(2)}) copy-start(f32[1280]{0:T(1024)} %param.8) | copy-start | bytes 15364
  0.0 42.1 %copy-start.7 = (f32[1280]{0:T(1024)S(1)}, f32[1280]{0:T(1024)}, u32[]{:S(2)}) copy-start(f32[1280]{0:T(1024)} %param.9) | copy-start | bytes 15364
  0.1 1.0 copy-start
  1.1 1.0 copy-start.2
  2.0 1.0 copy-start.4
  3.0 39.1 %copy-start.1 = (bf16[128,1280]{1,0:T(8,128)(2,1)S(1)}, bf16[128,1280]{1,0:T(8,128)(2,1)}, u32[]{:S(2)}) copy-start(bf16[128,1280]{1,0:T(8,128)(2,1)} %q_ref.1) | copy-start | bytes 983044
  3.0 39.1 %copy-start.3 = (bf16[128,1280]{1,0:T(8,128)(2,1)S(1)}, bf16[128,1280]{1,0:T(8,128)(2,1)}, u32[]{:S(2)}) copy-start(bf16[128,1280]{1,0:T(8,128)(2,1)} %k_ref.1) | copy-start | bytes 983044
  4.8 37.6 %copy-start.5 = (bf16[128,1280]{1,0:T(8,128)(2,1)S(1)}, bf16[128,1280]{1,0:T(8,128)(2,1)}, u32[]{:S(2)}) copy-start(bf16[128,1280]{1,0:T(8,128)(2,1)} %v_ref.1) | copy-start | bytes 983044
  4.8 38.6 %collective-permute-start = (bf16[128,1280]{1,0:T(8,128)(2,1)}, bf16[128,1280]{1,0:T(8,128)(2,1)S(1)}, u32[]{:S(2)}, u32[]{:S(2)}) collective-permute-start(bf16[128,1280]{1,0:T(8,128)(2,1)} %get-tuple-element.28), channel_id=1, source_target_pairs={{0,8},{8,16},{16,24},{24,0},{1,9},{9,17},{17,25},{25,1},{2,10},{10... | collective-permute-start | bytes 983048 | tf_op jit(solution)/shard_map/ppermute | solution.py:161
  9.2 34.2 %collective-permute-start.1 = (bf16[128,1280]{1,0:T(8,128)(2,1)}, bf16[128,1280]{1,0:T(8,128)(2,1)S(1)}, u32[]{:S(2)}, u32[]{:S(2)}) collective-permute-start(bf16[128,1280]{1,0:T(8,128)(2,1)} %get-tuple-element.29), channel_id=1, source_target_pairs={{0,16},{8,24},{16,0},{24,8},{1,17},{9,25},{17,1},{25,9},{2,18},{10... | collective-permute-start | bytes 983048 | tf_op jit(solution)/shard_map/ppermute | solution.py:161
  13.0 30.5 %collective-permute-start.2 = (bf16[128,1280]{1,0:T(8,128)(2,1)S(1)}, bf16[128,1280]{1,0:T(8,128)(2,1)S(1)}, u32[]{:S(2)}, u32[]{:S(2)}) collective-permute-start(bf16[128,1280]{1,0:T(8,128)(2,1)S(1)} %get-tuple-element.30), channel_id=1, source_target_pairs={{0,24},{8,0},{16,8},{24,16},{1,25},{9,1},{17,9},{25,17},{2,26},{10... | collective-permute-start | bytes 983048 | tf_op jit(solution)/shard_map/ppermute | solution.py:161
  43.4 39.7 %all-to-all-start = ((bf16[16,8,3840]{2,1,0:T(8,128)(2,1)}), bf16[16,8,3840]{2,1,0:T(8,128)(2,1)S(1)}, u32[]{:S(2)}, u32[]{:S(2)}) async-start(bf16[16,8,3840]{2,1,0:T(8,128)(2,1)} %bitcast.18), calls=%async_computation | async-start | bytes 1966080 | tf_op jit(solution)/shard_map/all_to_all | solution.py:168
  54.9 8.5 %copy-start.8 = (f32[1280]{0:T(1024)S(1)}, f32[1280]{0:T(1024)}, u32[]{:S(2)}) copy-start(f32[1280]{0:T(1024)} %param.9) | copy-start | bytes 15364
  55.7 9.3 %collective-permute-start.3 = (bf16[128,1408]{1,0:T(8,128)(2,1)}, bf16[128,1408]{1,0:T(8,128)(2,1)S(1)}, u32[]{:S(2)}, u32[]{:S(2)}) collective-permute-start(bf16[128,1408]{1,0:T(8,128)(2,1)} %pad_maximum_fusion.1), channel_id=1, source_target_pairs={{0,4},{4,0},{1,5},{5,1},{2,6},{6,2},{3,7},{7,3},{8,12},{12,8},{9,1... | collective-permute-start | bytes 1081352 | tf_op jit(solution)/shard_map/ppermute | solution.py:186
  58.3 5.1 %collective-permute-start.4 = (bf16[128,640]{1,0:T(8,128)(2,1)}, bf16[128,640]{1,0:T(8,128)(2,1)S(1)}, u32[]{:S(2)}, u32[]{:S(2)}) collective-permute-start(bf16[128,640]{1,0:T(8,128)(2,1)} %slice.30), channel_id=1, source_target_pairs={{0,4},{4,0},{1,5},{5,1},{2,6},{6,2},{3,7},{7,3},{8,12},{12,8},{9,1... | collective-permute-start | bytes 491528 | tf_op jit(solution)/shard_map/ppermute | solution.py:186
  61.4 3.6 %collective-permute-start.5 = (bf16[128,640]{1,0:T(8,128)(2,1)}, bf16[128,640]{1,0:T(8,128)(2,1)}, u32[]{:S(2)}, u32[]{:S(2)}) collective-permute-start(bf16[128,640]{1,0:T(8,128)(2,1)} %slice.31), channel_id=1, source_target_pairs={{0,4},{4,0},{1,5},{5,1},{2,6},{6,2},{3,7},{7,3},{8,12},{12,8},{9,1... | collective-permute-start | bytes 491528 | tf_op jit(solution)/shard_map/ppermute | solution.py:186
  69.5 16.9 %collective-permute-start.6 = (bf16[256,128]{1,0:T(8,128)(2,1)}, bf16[256,128]{1,0:T(8,128)(2,1)S(1)}, u32[]{:S(2)}, u32[]{:S(2)}) collective-permute-start(bf16[256,128]{1,0:T(8,128)(2,1)} %get-tuple-element.37), channel_id=1, source_target_pairs={{0,24},{8,0},{16,8},{24,16},{1,25},{9,1},{17,9},{25,17},{2,26},{10... | collective-permute-start | bytes 196616 | tf_op jit(solution)/shard_map/ppermute | solution.py:161
  71.4 15.0 %collective-permute-start.7 = (bf16[256,128]{1,0:T(8,128)(2,1)}, bf16[256,128]{1,0:T(8,128)(2,1)S(1)}, u32[]{:S(2)}, u32[]{:S(2)}) collective-permute-start(bf16[256,128]{1,0:T(8,128)(2,1)} %get-tuple-element.38), channel_id=1, source_target_pairs={{0,16},{8,24},{16,0},{24,8},{1,17},{9,25},{17,1},{25,9},{2,18},{10... | collective-permute-start | bytes 196616 | tf_op jit(solution)/shard_map/ppermute | solution.py:161
  77.4 9.0 %collective-permute-start.8 = (bf16[256,128]{1,0:T(8,128)(2,1)}, bf16[256,128]{1,0:T(8,128)(2,1)S(1)}, u32[]{:S(2)}, u32[]{:S(2)}) collective-permute-start(bf16[256,128]{1,0:T(8,128)(2,1)} %get-tuple-element.39), channel_id=1, source_target_pairs={{0,8},{8,16},{16,24},{24,0},{1,9},{9,17},{17,25},{25,1},{2,10},{10... | collective-permute-start | bytes 196616 | tf_op jit(solution)/shard_map/ppermute | solution.py:161
  86.5 22.8 %all-to-all-start.1 = ((bf16[16,8,1280]{2,1,0:T(8,128)(2,1)}), bf16[16,8,1280]{2,1,0:T(8,128)(2,1)S(1)}, u32[]{:S(2)}, u32[]{:S(2)}) async-start(bf16[16,8,1280]{2,1,0:T(8,128)(2,1)} %bitcast.9), calls=%async_computation.1 | async-start | bytes 655360 | tf_op jit(solution)/shard_map/all_to_all | solution.py:168
  94.8 3.3 %collective-permute-start.9 = (bf16[128,640]{1,0:T(8,128)(2,1)S(1)}, bf16[128,640]{1,0:T(8,128)(2,1)S(1)}, u32[]{:S(2)}, u32[]{:S(2)}) collective-permute-start(bf16[128,640]{1,0:T(8,128)(2,1)S(1)} %get-tuple-element.48), channel_id=1, source_target_pairs={{0,4},{4,0},{1,5},{5,1},{2,6},{6,2},{3,7},{7,3},{8,12},{12,8},{9,1... | collective-permute-start | bytes 491528 | tf_op jit(solution)/shard_map/ppermute | solution.py:207

commit v4 on v3

--- a/solution.py
+++ b/solution.py
@@ -32,22 +32,36 @@
     return (x.astype(jnp.float32) * scale * gain).astype(jnp.bfloat16)
 
 
-def prep_kernel(at_ref, q_ref, k_ref, v_ref, p0, p1, p2, p3, sum_ref):
-    n, width = q_ref.shape
+def prep_kernel(at_ref, q_hbm, k_hbm, v_hbm, p0, p1, p2, p3, keep_ref, sum_ref, x_ref, sems):
+    n, width = q_hbm.shape
+    loads = []
+    for i, src in enumerate((q_hbm, k_hbm, v_hbm)):
+        for r in range(2):
+            rows = pl.ds(r * (n // 2), n // 2)
+            dst = x_ref.at[rows, pl.ds(i * width, width)]
+            loads.append(pltpu.make_async_copy(src.at[rows], dst, sems.at[i * 2 + r]))
+    for load in loads:
+        load.start()
+    for load in loads:
+        load.wait()
     half = width // 2
     for j, out in enumerate((p0, p1, p2, p3)):
         h = lax.rem(at_ref[0] + j, 4) * HEAD
         for c, side in enumerate((at_ref[1], 1 - at_ref[1])):
-            moving = pl.ds(pl.multiple_of(side * half + h, HEAD), HEAD)
-            staying = pl.ds(pl.multiple_of((side + 1) * half - HEAD, HEAD), HEAD)
-            parts = ((q_ref, moving), (k_ref, moving), (v_ref, moving), (k_ref, staying), (v_ref, staying))
-            for i, (ref, col) in enumerate(parts):
-                out[:, c * half + i * HEAD : c * half + (i + 1) * HEAD] = ref[:, col]
+            moving, staying = side * half + h, (side + 1) * half - HEAD
+            five = ((0, moving), (1, moving), (2, moving), (1, staying), (2, staying))
+            for i, (a, start) in enumerate(five):
+                col = pl.ds(pl.multiple_of(a * width + start, HEAD), HEAD)
+                out[:, c * half + i * HEAD : c * half + (i + 1) * HEAD] = x_ref[:, col]
+    for c, side in enumerate((at_ref[1], 1 - at_ref[1])):
+        staying = pl.ds(pl.multiple_of((side + 1) * half - HEAD, HEAD), HEAD)
+        keep_ref[:, c * HEAD : (c + 1) * HEAD] = x_ref[:, staying]
     ones = jnp.ones((4, HEAD), jnp.float32)
-    for i, ref in enumerate((q_ref, k_ref)):
+    for i in range(2):
         total = jnp.zeros((n, HEAD), jnp.float32)
         for h in range(width // HEAD):
-            total += jnp.square(ref[:, h * HEAD : (h + 1) * HEAD].astype(jnp.float32))
+            start = i * width + h * HEAD
+            total += jnp.square(x_ref[:, start : start + HEAD].astype(jnp.float32))
         sum_ref[i * 4 : (i + 1) * 4, :] = lax.dot_general(
             ones,
             total,
@@ -62,15 +76,64 @@
     return pl.pallas_call(
         prep_kernel,
         out_shape=[jax.ShapeDtypeStruct(q.shape, q.dtype)] * 4
-        + [jax.ShapeDtypeStruct((8, q.shape[0]), jnp.float32)],
-        in_specs=[pl.BlockSpec(memory_space=pltpu.SMEM)] + [vmem] * 3,
-        out_specs=[vmem] * 5,
+        + [
+            jax.ShapeDtypeStruct((q.shape[0], 2 * HEAD), q.dtype),
+            jax.ShapeDtypeStruct((8, q.shape[0]), jnp.float32),
+            jax.ShapeDtypeStruct((q.shape[0], 3 * q.shape[1]), q.dtype),
+        ],
+        in_specs=[pl.BlockSpec(memory_space=pltpu.SMEM)] + [pl.BlockSpec(memory_space=pltpu.HBM)] * 3,
+        out_specs=[vmem] * 7,
+        scratch_shapes=[pltpu.SemaphoreType.DMA((6,))],
         compiler_params=pltpu.CompilerParams(vmem_limit_bytes=24 << 20),
         cost_estimate=pl.CostEstimate(flops=q.size * 4, bytes_accessed=q.size * 14, transcendentals=0),
     )(at, q, k, v)
 
 
-def spatial_kernel(at_ref, b0, b1, b2, b3, q_last, s0, s2, s3, stat_ref, qg_ref, kg_ref, o0, o1, o2, o3, o_last, q_all, k_all, v_all):
+def norm_kernel(x_ref, sum_ref, qg_ref, kg_ref, t_ref):
+    n, width = x_ref.shape[0], x_ref.shape[1] // 3
+    for i, gain in enumerate((qg_ref, kg_ref)):
+        stat = jnp.broadcast_to(sum_ref[i * 4 : i * 4 + 1, :], (n, n)).T
+        scale = lax.rsqrt(stat / D + EPS)
+        for h in range(width // HEAD):
+            here = slice(i * width + h * HEAD, i * width + (h + 1) * HEAD)
+            value = x_ref[:, here].astype(jnp.float32) * scale * gain[:, h * HEAD : (h + 1) * HEAD]
+            t_ref[:, here] = value.astype(jnp.bfloat16)
+    t_ref[:, 2 * width :] = x_ref[:, 2 * width :]
+
+
+def norm(x, sums, q_gain, k_gain):
+    vmem = pl.BlockSpec(memory_space=pltpu.VMEM)
+    return pl.pallas_call(
+        norm_kernel,
+        out_shape=jax.ShapeDtypeStruct(x.shape, x.dtype),
+        in_specs=[vmem] * 4,
+        out_specs=vmem,
+        compiler_params=pltpu.CompilerParams(vmem_limit_bytes=24 << 20),
+        cost_estimate=pl.CostEstimate(flops=x.size * 3, bytes_accessed=x.size * 4, transcendentals=0),
+    )(x, sums, q_gain, k_gain)
+
+
+def pack_kernel(b0, b1, b2, b3, keep, out):
+    half = b0.shape[1] // 2
+    for j, blk in enumerate((b0, b1, b2, b3)):
+        out[:, j * half : (j + 1) * half] = blk[:, half:]
+    out[:, 4 * half :] = keep[:, HEAD:]
+
+
+def pack(blocks, keep):
+    n, width = blocks[0].shape
+    vmem = pl.BlockSpec(memory_space=pltpu.VMEM)
+    return pl.pallas_call(
+        pack_kernel,
+        out_shape=jax.ShapeDtypeStruct((n, 2 * width + HEAD), keep.dtype),
+        in_specs=[vmem] * 5,
+        out_specs=vmem,
+        compiler_params=pltpu.CompilerParams(vmem_limit_bytes=24 << 20),
+        cost_estimate=pl.CostEstimate(flops=0, bytes_accessed=n * width * 8, transcendentals=0),
+    )(*blocks, keep)
+
+
+def spatial_kernel(at_ref, b0, b1, b2, b3, keep, sw_ref, stat_ref, qg_ref, kg_ref, o0, o1, o2, o3, o_last, q_all, k_all, v_all):
     n, half = b0.shape[0], b0.shape[1] // 2
     zl, core = at_ref[0], at_ref[1]
     moving = pl.ds(pl.multiple_of(core * half + zl * HEAD, HEAD), HEAD)
@@ -82,8 +145,7 @@
 
             def part(i):
                 if twin:
-                    ref, at = ((s0, 0), (s0, half), (s2, 0), (s3, 0))[j]
-                    return ref[:, at + i * HEAD : at + (i + 1) * HEAD]
+                    return sw_ref[:, j * half + i * HEAD : j * half + (i + 1) * HEAD]
                 return blk[:, i * HEAD : (i + 1) * HEAD]
 
             rows = slice((j * 2 + twin) * n, (j * 2 + twin + 1) * n)
@@ -96,7 +158,7 @@
             k_all[rows, HEAD:] = normed(part(3), k_stat, k_gain_last)
             v_all[rows, HEAD:] = part(4)
             if j == 0:
-                q = s0[:, 2 * half :] if twin else q_last[...]
+                q = sw_ref[:, 4 * half :] if twin else keep[:, 0:HEAD]
                 q_all[rows, HEAD:] = normed(q, q_stat, q_gain_last)
     k_one, k_two = k_all[:, 0:HEAD], k_all[:, HEAD:]
     v_one, v_two = v_all[:, 0:HEAD], v_all[:, HEAD:]
@@ -106,20 +168,20 @@
     o_last[...] = softmax_times(contract_last(q_all[0 : 2 * n, HEAD:], k_two), v_two).astype(jnp.bfloat16)
 
 
-def spatial(at, blocks, q_last, swapped, stats, q_gain, k_gain):
+def spatial(at, blocks, keep, swapped, stats, q_gain, k_gain):
     n = blocks[0].shape[0]
     vmem = pl.BlockSpec(memory_space=pltpu.VMEM)
     return pl.pallas_call(
         spatial_kernel,
         out_shape=[jax.ShapeDtypeStruct((2 * n, HEAD), jnp.bfloat16)] * 5,
-        in_specs=[pl.BlockSpec(memory_space=pltpu.SMEM)] + [vmem] * 11,
+        in_specs=[pl.BlockSpec(memory_space=pltpu.SMEM)] + [vmem] * 9,
         out_specs=[vmem] * 5,
         scratch_shapes=[pltpu.VMEM((8 * n, 2 * HEAD), jnp.bfloat16)] * 3,
         compiler_params=pltpu.CompilerParams(vmem_limit_bytes=40 << 20),
         cost_estimate=pl.CostEstimate(
             flops=5 * n * n * 64 * HEAD, bytes_accessed=n * HEAD * 120, transcendentals=5 * n * n * 16
         ),
-    )(at, *blocks, q_last, *swapped, stats, q_gain, k_gain)
+    )(at, *blocks, keep, swapped, stats, q_gain, k_gain)
 
 
 def temporal_kernel(x_ref, out_ref, *, per):
@@ -168,28 +230,21 @@
         return lax.all_to_all(sent, FRAME, 0, 0, tiled=True).reshape(a.shape)
 
     at = jnp.stack([zl, core])
-    *parts, sums = prep(at, queries, keys, values)
+    *parts, keep, sums, three = prep(at, queries, keys, values)
     blocks = [parts[0]] + [shift(parts[j], j) for j in (1, 2, 3)]
     sums = lax.psum(sums, "tp")
 
-    q_norm = normed(queries, sums[0][:, None], query_gain[None, :])
-    k_norm = normed(keys, sums[4][:, None], key_gain[None, :])
-    t_sent = jnp.concatenate([q_norm, k_norm, values], axis=1)
+    t_sent = norm(three, sums, query_gain[None], key_gain[None])
     stat = jnp.stack([sums[0], sums[4]])
     stats = lax.all_gather(stat, ("zl", "c")).transpose(0, 2, 1).reshape(8 * tok, 2)
     t_sent, blocks, stats = lax.optimization_barrier((t_sent, blocks, stats))
     t_in = to_positions(t_sent)
 
-    away = [b[:, half:] for b in blocks]
-    q_away = column(queries, (2 - core) * half - HEAD)
-    swapped = [
-        lax.ppermute(a, "c", swap)
-        for a in (jnp.concatenate([away[0], away[1], q_away], axis=1), away[2], away[3])
-    ]
+    swapped = lax.ppermute(pack(blocks, keep), "c", swap)
     outs = spatial(
         at,
         blocks,
-        column(queries, (core + 1) * half - HEAD),
+        keep,
         swapped,
         stats,
         query_gain[None],
@@ -200,7 +255,7 @@
     t_back = to_positions(t_out)
 
     moved = [shift(outs[j], 4 - j) for j in (1, 2, 3)]
-    moved, t_out = lax.optimization_barrier((moved, t_out))
+    moved = lax.optimization_barrier((moved, t_out))[0]
     heads = [outs[0]] + moved
     turned = column(jnp.concatenate(heads + heads[:3], axis=1), (4 - zl) % 4 * HEAD, 4 * HEAD)
     s_half = jnp.concatenate([turned, last], axis=1)

time: 111 us -> 106 us (0.955)
  the two profiles are of different devices: /device:TPU:80 before, /device:TPU:16 now
where the time goes in v4:
time: 106 us
  starting transfers between devices  51.9 us (49%)
  blocking collectives  21.1 us (20%)
  waiting for transfers between devices  13.4 us (13%)
  Pallas kernels  11.6 us (11%)
  local copies, waits for them, and re-layouts  6.39 us (6%)
    ppermute x6, starting transfers between devices, shift(): return lax.ppermute(a, 'zl', [(i, (i + j) % 4) for i in range(4)])  28.2 us
    all_to_all x2, starting transfers between devices, to_positions(): return lax.all_to_all(sent, FRAME, 0, 0, tiled=True).reshape(a.shape)  19.9 us
    psum x1, blocking collectives, per_device(): sums = lax.psum(sums, 'tp')  11.2 us
    all_gather x1, blocking collectives, per_device(): lax.all_gather(stat, ('zl', 'c')).transpose(0, 2, 1).reshape(8 * tok, 2)  9.87 us
    all_to_all x2, waiting for transfers between devices, to_positions(): return lax.all_to_all(sent, FRAME, 0, 0, tiled=True).reshape(a.shape)  9.72 us
    unnamed x28, local copies, waits for them, and re-layouts  6.11 us
    pallas_call x1, Pallas kernels, spatial(): pl.pallas_call(spatial_kernel, out_shape=[jax.ShapeDtypeStruct((2 * n, HE...  4.07 us
    pallas_call x1, Pallas kernels, temporal(): pl.pallas_call(lambda *refs: temporal_kernel(*refs, per=per), out_shape=j...  3.23 us
  transfers between devices with their start and end apart: 10, of which 4 were waited for; matrix products, arithmetic and copies ran while one was open for 0% of the time, Pallas kernels for 9%

profile of v4, /device:TPU:16, one launch (start us, length us, event | category | flops | bytes accessed | tf_op | source)
XLA Modules:
  0.0 105.6 jit_solution(2672988596857979731)
XLA Ops:
  0.0 0.1 pad_add_fusion.at_ref
  0.1 1.0 copy-done
  1.1 1.0 copy-done.1
  2.0 1.0 copy-done.2
  3.0 2.0 %shard_map.55 = (bf16[128,1280]{1,0:T(8,128)(2,1)S(1)}, bf16[128,1280]{1,0:T(8,128)(2,1)}, bf16[128,1280]{1,0:T(8,128)(2,1)}, bf16[128,1280]{1,0:T(8,128)(2,1)S(...) custom-call(s32[2]{0:T(128)S(1)} %pad_add_fusion.at_ref, ...), custom_call_target="tpu_custom_call" | custom-call | flops 655360 | bytes 2293760 | tf_op jit(solution)/shard_map/pallas_call | solution.py:76
  5.1 0.0 copy-start.10
  5.1 4.4 %collective-permute-start = (bf16[128,1280]{1,0:T(8,128)(2,1)}, bf16[128,1280]{1,0:T(8,128)(2,1)S(1)}, u32[]{:S(2)}, u32[]{:S(2)}) collective-permute-start(bf16[128,1280]{1,0:T(8,128)(2,1)} %get-tuple-element.31), channel_id=1, source_target_pairs={{0,8},{8,16},{16,24},{24,0},{1,9},{9,17},{17,25},{25,1},{2,10},{10... | collective-permute-start | bytes 983048 | tf_op jit(solution)/shard_map/ppermute | solution.py:223
  9.5 6.1 %collective-permute-start.1 = (bf16[128,1280]{1,0:T(8,128)(2,1)}, bf16[128,1280]{1,0:T(8,128)(2,1)S(1)}, u32[]{:S(2)}, u32[]{:S(2)}) collective-permute-start(bf16[128,1280]{1,0:T(8,128)(2,1)} %get-tuple-element.32), channel_id=1, source_target_pairs={{0,16},{8,24},{16,0},{24,8},{1,17},{9,25},{17,1},{25,9},{2,18},{10... | collective-permute-start | bytes 983048 | tf_op jit(solution)/shard_map/ppermute | solution.py:223
  15.6 2.5 %collective-permute-start.2 = (bf16[128,1280]{1,0:T(8,128)(2,1)S(1)}, bf16[128,1280]{1,0:T(8,128)(2,1)S(1)}, u32[]{:S(2)}, u32[]{:S(2)}) collective-permute-start(bf16[128,1280]{1,0:T(8,128)(2,1)S(1)} %get-tuple-element.33), channel_id=1, source_target_pairs={{0,24},{8,0},{16,8},{24,16},{1,25},{9,1},{17,9},{25,17},{2,26},{10... | collective-permute-start | bytes 983048 | tf_op jit(solution)/shard_map/ppermute | solution.py:223
  18.1 11.2 %psum.7.sum_ref = f32[8,128]{1,0:T(8,128)S(1)} all-reduce(f32[8,128]{1,0:T(8,128)S(1)} %get-tuple-element.29), channel_id=1, replica_groups=mesh['x'=4,'yl'=2,'zh'=2,'zl'=4,'c'=2,'tp'=4] {'tp'}, use_global_device_ids=true, to_apply=%region_0.0 | all-reduce | flops 1024 | bytes 8192 | tf_op jit(solution)/shard_map/psum | solution.py:235
  29.3 9.9 %all-gather.1 = f32[8,2,128]{2,1,0:T(2,128)S(1)} all-gather(f32[1,2,128]{2,1,0:T(2,128)S(1)} %maximum_bitcast_fusion), channel_id=2, replica_groups=mesh['x'=4,'yl'=2,'zh'=2,'zl'=4,'c'=2,'tp'=4] {'zl','c'}, dimensions={0}, use_global_device_ids=true | all-gather | bytes 9216 | tf_op jit(solution)/shard_map/all_gather | solution.py:239
  39.2 0.2 copy.7
  39.4 1.3 %shard_map.56 = bf16[128,3840]{1,0:T(8,128)(2,1)} custom-call(bf16[128,3840]{1,0:T(8,128)(2,1)S(1)} %get-tuple-element.28.x_ref, f32[8,128]{1,0:T(8,128)S(1)} %psum.7.sum_ref, f32[1,1280]{1,0:T(1,128)S(1)} %broadcast_in_dim.8.qg_ref, f32[1,1280]{1,0:T(1,128)S(1)} %broadcast_in_dim.9.kg_ref), custom_call_target="tpu_custom_call" | custom-call | flops 1474560 | bytes 1966080 | tf_op jit(solution)/shard_map/pallas_call | solution.py:106
  40.7 11.3 %all-to-all-start = ((bf16[16,8,3840]{2,1,0:T(8,128)(2,1)}), bf16[16,8,3840]{2,1,0:T(8,128)(2,1)S(1)}, u32[]{:S(2)}, u32[]{:S(2)}) async-start(bf16[16,8,3840]{2,1,0:T(8,128)(2,1)} %bitcast.5), calls=%async_computation | async-start | bytes 1966080 | tf_op jit(solution)/shard_map/all_to_all | solution.py:230
  52.0 1.0 shard_map.57
  53.0 1.9 %collective-permute-start.3 = (bf16[128,2688]{1,0:T(8,128)(2,1)}, bf16[128,2688]{1,0:T(8,128)(2,1)S(1)}, u32[]{:S(2)}, u32[]{:S(2)}) collective-permute-start(bf16[128,2688]{1,0:T(8,128)(2,1)} %shard_map.57), channel_id=1, source_target_pairs={{0,4},{4,0},{1,5},{5,1},{2,6},{6,2},{3,7},{7,3},{8,12},{12,8},{9,1... | collective-permute-start | bytes 2064392 | tf_op jit(solution)/shard_map/ppermute | solution.py:243
  54.9 2.3 %collective-permute-done.3.sw_ref = bf16[128,2688]{1,0:T(8,128)(2,1)S(1)} collective-permute-done((bf16[128,2688]{1,0:T(8,128)(2,1)}, bf16[128,2688]{1,0:T(8,128)(2,1)S(1)}, u32[]{:S(2)}, u32[]{:S(2)}) %collective-permute-start.3) | collective-permute-done | bytes 688160 | tf_op jit(solution)/shard_map/ppermute | solution.py:243
  57.2 0.8 copy-done.4
  58.0 4.1 %shard_map.58 = (bf16[256,128]{1,0:T(8,128)(2,1)S(1)}, bf16[256,128]{1,0:T(8,128)(2,1)}, bf16[256,128]{1,0:T(8,128)(2,1)}, bf16[256,128]{1,0:T(8,128)(2,1)}, bf16[256,128]{1,0:T(8,128)(2,1)S(1)}) custom-call(s32[2]{0:T(128)S(1)} %pad_add_fusion.at_ref, bf16[128,1280]{1,0:T(8,128)(2,1)S(1)} %get-tuple-element.34.b0, ...), custom_call_target="tpu_custom_call" | custom-call | flops 671088640 | bytes 1966080 | tf_op jit(solution)/shard_map/pallas_call | solution.py:174
  62.1 0.6 copy-done.7
  62.7 9.3 %collective-permute-start.4 = (bf16[256,128]{1,0:T(8,128)(2,1)}, bf16[256,128]{1,0:T(8,128)(2,1)S(1)}, u32[]{:S(2)}, u32[]{:S(2)}) collective-permute-start(bf16[256,128]{1,0:T(8,128)(2,1)} %get-tuple-element.41), channel_id=1, source_target_pairs={{0,24},{8,0},{16,8},{24,16},{1,25},{9,1},{17,9},{25,17},{2,26},{10... | collective-permute-start | bytes 196616 | tf_op jit(solution)/shard_map/ppermute | solution.py:223
  72.1 2.0 %collective-permute-start.5 = (bf16[256,128]{1,0:T(8,128)(2,1)}, bf16[256,128]{1,0:T(8,128)(2,1)S(1)}, u32[]{:S(2)}, u32[]{:S(2)}) collective-permute-start(bf16[256,128]{1,0:T(8,128)(2,1)} %get-tuple-element.42), channel_id=1, source_target_pairs={{0,16},{8,24},{16,0},{24,8},{1,17},{9,25},{17,1},{25,9},{2,18},{10... | collective-permute-start | bytes 196616 | tf_op jit(solution)/shard_map/ppermute | solution.py:223
  74.1 3.9 %collective-permute-start.6 = (bf16[256,128]{1,0:T(8,128)(2,1)}, bf16[256,128]{1,0:T(8,128)(2,1)S(1)}, u32[]{:S(2)}, u32[]{:S(2)}) collective-permute-start(bf16[256,128]{1,0:T(8,128)(2,1)} %get-tuple-element.43), channel_id=1, source_target_pairs={{0,8},{8,16},{16,24},{24,0},{1,9},{9,17},{17,25},{25,1},{2,10},{10... | collective-permute-start | bytes 196616 | tf_op jit(solution)/shard_map/ppermute | solution.py:223
  78.0 1.9 %all-to-all-done = bf16[16,8,3840]{2,1,0:T(8,128)(2,1)S(1)} async-done(((bf16[16,8,3840]{2,1,0:T(8,128)(2,1)}), bf16[16,8,3840]{2,1,0:T(8,128)(2,1)S(1)}, u32[]{:S(2)}, u32[]{:S(2)}) %all-to-all-start) | async-done | bytes 983072 | tf_op jit(solution)/shard_map/all_to_all | solution.py:230
  80.0 3.2 %shard_map.59 = bf16[128,1280]{1,0:T(8,128)(2,1)} custom-call(bf16[128,3840]{1,0:T(8,128)(2,1)S(1)} %bitcast.12), custom_call_target="tpu_custom_call" | custom-call | flops 83886080 | bytes 1310720 | tf_op jit(solution)/shard_map/pallas_call | solution.py:203
  83.2 8.6 %all-to-all-start.1 = ((bf16[16,8,1280]{2,1,0:T(8,128)(2,1)}), bf16[16,8,1280]{2,1,0:T(8,128)(2,1)S(1)}, u32[]{:S(2)}, u32[]{:S(2)}) async-start(bf16[16,8,1280]{2,1,0:T(8,128)(2,1)} %bitcast.7), calls=%async_computation.1 | async-start | bytes 655360 | tf_op jit(solution)/shard_map/all_to_all | solution.py:230
  91.9 0.8 copy-done.6
  92.8 0.8 copy-done.8
  93.7 1.9 %collective-permute-start.7 = (bf16[128,640]{1,0:T(8,128)(2,1)S(1)}, bf16[128,640]{1,0:T(8,128)(2,1)S(1)}, u32[]{:S(2)}, u32[]{:S(2)}) collective-permute-start(bf16[128,640]{1,0:T(8,128)(2,1)S(1)} %get-tuple-element.52), channel_id=1, source_target_pairs={{0,4},{4,0},{1,5},{5,1},{2,6},{6,2},{3,7},{7,3},{8,12},{12,8},{9,1... | collective-permute-start | bytes 491528 | tf_op jit(solution)/shard_map/ppermute | solution.py:262
  95.6 1.4 %collective-permute-done.7 = bf16[128,640]{1,0:T(8,128)(2,1)S(1)} collective-permute-done((bf16[128,640]{1,0:T(8,128)(2,1)S(1)}, bf16[128,640]{1,0:T(8,128)(2,1)S(1)}, u32[]{:S(2)}, u32[]{:S(2)}) %collective-permute-start.7) | collective-permute-done | bytes 163872 | tf_op jit(solution)/shard_map/ppermute | solution.py:262
  96.9 7.8 %all-to-all-done.1 = bf16[16,8,1280]{2,1,0:T(8,128)(2,1)S(1)} async-done(((bf16[16,8,1280]{2,1,0:T(8,128)(2,1)}), bf16[16,8,1280]{2,1,0:T(8,128)(2,1)S(1)}, u32[]{:S(2)}, u32[]{:S(2)}) %all-to-all-start.1) | async-done | bytes 327712 | tf_op jit(solution)/shard_map/all_to_all | solution.py:230
  104.7 0.8 fusion
  (33 shorter events, 0.3 us)
Async XLA Ops:
  0.1 1.0 copy-start
  1.0 1.0 copy-start.1
  2.0 1.0 copy-start.2
  3.0 15.1 %copy-start.9 = (f32[1280]{0:T(1024)S(1)}, f32[1280]{0:T(1024)}, u32[]{:S(2)}) copy-start(f32[1280]{0:T(1024)} %param.8) | copy-start | bytes 15364
  5.0 47.0 %copy-start.3 = (bf16[128,256]{1,0:T(8,128)(2,1)}, bf16[128,256]{1,0:T(8,128)(2,1)S(1)}, u32[]{:S(2)}) copy-start(bf16[128,256]{1,0:T(8,128)(2,1)S(1)} %get-tuple-element.38.keep) | copy-start | bytes 196612
  5.1 13.0 %copy-start.10 = (f32[1280]{0:T(1024)S(1)}, f32[1280]{0:T(1024)}, u32[]{:S(2)}) copy-start(f32[1280]{0:T(1024)} %param.9) | copy-start | bytes 15364
  5.1 35.6 %collective-permute-start = (bf16[128,1280]{1,0:T(8,128)(2,1)}, bf16[128,1280]{1,0:T(8,128)(2,1)S(1)}, u32[]{:S(2)}, u32[]{:S(2)}) collective-permute-start(bf16[128,1280]{1,0:T(8,128)(2,1)} %get-tuple-element.31), channel_id=1, source_target_pairs={{0,8},{8,16},{16,24},{24,0},{1,9},{9,17},{17,25},{25,1},{2,10},{10... | collective-permute-start | bytes 983048 | tf_op jit(solution)/shard_map/ppermute | solution.py:223
  9.5 31.2 %collective-permute-start.1 = (bf16[128,1280]{1,0:T(8,128)(2,1)}, bf16[128,1280]{1,0:T(8,128)(2,1)S(1)}, u32[]{:S(2)}, u32[]{:S(2)}) collective-permute-start(bf16[128,1280]{1,0:T(8,128)(2,1)} %get-tuple-element.32), channel_id=1, source_target_pairs={{0,16},{8,24},{16,0},{24,8},{1,17},{9,25},{17,1},{25,9},{2,18},{10... | collective-permute-start | bytes 983048 | tf_op jit(solution)/shard_map/ppermute | solution.py:223
  15.6 25.1 %collective-permute-start.2 = (bf16[128,1280]{1,0:T(8,128)(2,1)S(1)}, bf16[128,1280]{1,0:T(8,128)(2,1)S(1)}, u32[]{:S(2)}, u32[]{:S(2)}) collective-permute-start(bf16[128,1280]{1,0:T(8,128)(2,1)S(1)} %get-tuple-element.33), channel_id=1, source_target_pairs={{0,24},{8,0},{16,8},{24,16},{1,25},{9,1},{17,9},{25,17},{2,26},{10... | collective-permute-start | bytes 983048 | tf_op jit(solution)/shard_map/ppermute | solution.py:223
  40.7 39.2 %all-to-all-start = ((bf16[16,8,3840]{2,1,0:T(8,128)(2,1)}), bf16[16,8,3840]{2,1,0:T(8,128)(2,1)S(1)}, u32[]{:S(2)}, u32[]{:S(2)}) async-start(bf16[16,8,3840]{2,1,0:T(8,128)(2,1)} %bitcast.5), calls=%async_computation | async-start | bytes 1966080 | tf_op jit(solution)/shard_map/all_to_all | solution.py:230
  53.0 4.2 %collective-permute-start.3 = (bf16[128,2688]{1,0:T(8,128)(2,1)}, bf16[128,2688]{1,0:T(8,128)(2,1)S(1)}, u32[]{:S(2)}, u32[]{:S(2)}) collective-permute-start(bf16[128,2688]{1,0:T(8,128)(2,1)} %shard_map.57), channel_id=1, source_target_pairs={{0,4},{4,0},{1,5},{5,1},{2,6},{6,2},{3,7},{7,3},{8,12},{12,8},{9,1... | collective-permute-start | bytes 2064392 | tf_op jit(solution)/shard_map/ppermute | solution.py:243
  57.2 0.8 copy-start.4
  62.1 0.6 copy-start.7
  62.7 15.3 %copy-start.5 = (bf16[256,128]{1,0:T(8,128)(2,1)}, bf16[256,128]{1,0:T(8,128)(2,1)S(1)}, u32[]{:S(2)}) copy-start(bf16[256,128]{1,0:T(8,128)(2,1)S(1)} %get-tuple-element.40) | copy-start | bytes 196612
  62.7 29.1 %collective-permute-start.4 = (bf16[256,128]{1,0:T(8,128)(2,1)}, bf16[256,128]{1,0:T(8,128)(2,1)S(1)}, u32[]{:S(2)}, u32[]{:S(2)}) collective-permute-start(bf16[256,128]{1,0:T(8,128)(2,1)} %get-tuple-element.41), channel_id=1, source_target_pairs={{0,24},{8,0},{16,8},{24,16},{1,25},{9,1},{17,9},{25,17},{2,26},{10... | collective-permute-start | bytes 196616 | tf_op jit(solution)/shard_map/ppermute | solution.py:223
  72.1 19.7 %collective-permute-start.5 = (bf16[256,128]{1,0:T(8,128)(2,1)}, bf16[256,128]{1,0:T(8,128)(2,1)S(1)}, u32[]{:S(2)}, u32[]{:S(2)}) collective-permute-start(bf16[256,128]{1,0:T(8,128)(2,1)} %get-tuple-element.42), channel_id=1, source_target_pairs={{0,16},{8,24},{16,0},{24,8},{1,17},{9,25},{17,1},{25,9},{2,18},{10... | collective-permute-start | bytes 196616 | tf_op jit(solution)/shard_map/ppermute | solution.py:223
  74.1 17.7 %collective-permute-start.6 = (bf16[256,128]{1,0:T(8,128)(2,1)}, bf16[256,128]{1,0:T(8,128)(2,1)S(1)}, u32[]{:S(2)}, u32[]{:S(2)}) collective-permute-start(bf16[256,128]{1,0:T(8,128)(2,1)} %get-tuple-element.43), channel_id=1, source_target_pairs={{0,8},{8,16},{16,24},{24,0},{1,9},{9,17},{17,25},{25,1},{2,10},{10... | collective-permute-start | bytes 196616 | tf_op jit(solution)/shard_map/ppermute | solution.py:223
  83.2 21.6 %all-to-all-start.1 = ((bf16[16,8,1280]{2,1,0:T(8,128)(2,1)}), bf16[16,8,1280]{2,1,0:T(8,128)(2,1)S(1)}, u32[]{:S(2)}, u32[]{:S(2)}) async-start(bf16[16,8,1280]{2,1,0:T(8,128)(2,1)} %bitcast.7), calls=%async_computation.1 | async-start | bytes 655360 | tf_op jit(solution)/shard_map/all_to_all | solution.py:230
  91.9 0.8 copy-start.6
  92.8 0.8 copy-start.8
  93.7 3.3 %collective-permute-start.7 = (bf16[128,640]{1,0:T(8,128)(2,1)S(1)}, bf16[128,640]{1,0:T(8,128)(2,1)S(1)}, u32[]{:S(2)}, u32[]{:S(2)}) collective-permute-start(bf16[128,640]{1,0:T(8,128)(2,1)S(1)} %get-tuple-element.52), channel_id=1, source_target_pairs={{0,4},{4,0},{1,5},{5,1},{2,6},{6,2},{3,7},{7,3},{8,12},{12,8},{9,1... | collective-permute-start | bytes 491528 | tf_op jit(solution)/shard_map/ppermute | solution.py:262
